TPU v7x, 256 devices: a whole 4x4x8 slice. The times are simulated.
256 devices in a mesh: dp: 32 (over z, x), tensor: 8 (over y, core).
Axes of the slice: x: 4, y: 4, z: 8, core: 2. Of those that a mesh axis runs over, the one named last changes fastest.
Arguments:
- queries: bfloat16 [8192, 3072], P('dp', 'tensor'), may hold values from -100 to 100
- keys: bfloat16 [8192, 3072], P('dp', 'tensor'), may hold values from -8 to 8
- values: bfloat16 [8192, 3072], P('dp', 'tensor'), may hold values from -6 to 6
- upstream: bfloat16 [8192, 6144], P('dp', 'tensor'), may hold values from -6 to 6
- out_weight: bfloat16 [6144, 3072], P('dp', 'tensor'), may hold values from -0.109375 to 0.109375
- fisher: float32 [6144, 3072], P('dp', 'tensor'), may hold values from 0.02 to 0.2
- image_lengths: int32 [32, 8], P('dp'), may hold values from 1 to 128, as said below
Outputs:
- grad_queries: bfloat16 [8192, 3072], P('dp', 'tensor')
- grad_keys: bfloat16 [8192, 3072], P('dp', 'tensor')
- grad_values: bfloat16 [8192, 3072], P('dp', 'tensor')
- weight_grad: float32 [6144, 3072], P('dp', 'tensor')
- fisher_next: float32 [6144, 3072], P('dp', 'tensor')
Inputs may be any that keep to these rules, and one draw needn't show every extreme that they name: `image_lengths`: each row lists the patch counts of 8 images packed one after another from the first slot of a sequence; a row sums to at most 256, and in every draw some row sums to exactly 256. No image has more than 128 patches, and in every draw some image has exactly that many.
All inputs are finite; a program needn't handle non-finite values.
Results may differ from a plain program's by a relative error of at most 0.028.
Values may be sent and summed in bfloat16 or wider, within the bound.
A program may use at most 64 MiB of HBM per device.

v0:
```python
import jax
import jax.numpy as jnp
from jax import lax
from jax.sharding import PartitionSpec as P

HD = 128


FLOOR_SCORE = -1e30


def per_device(queries, keys, values, upstream, out_weight, fisher, image_lengths):
    slot_count = queries.shape[0]
    local_width = queries.shape[1]
    heads_here = local_width // HD
    score_scale = HD ** (-0.5)
    query_span = min(512, slot_count)
    key_span = min(128, slot_count)
    lengths = image_lengths[0]
    finish = jnp.cumsum(lengths)
    positions = jnp.arange(slot_count, dtype=jnp.int32)
    segment = jnp.sum((positions[:, None] >= finish[None, :]).astype(jnp.int32), axis=1)
    filled = finish[-1]
    inside = positions < filled
    whole = lax.all_gather(upstream, "tensor", axis=1, tiled=True)
    grad_masked = jnp.where(inside[:, None], whole, jnp.zeros_like(whole))
    grad_attn = jnp.dot(
        grad_masked,
        lax.all_gather(out_weight, "dp", axis=0, tiled=True),
        preferred_element_type=jnp.float32,
    ).astype(jnp.bfloat16)
    query_heads = queries.reshape(slot_count, heads_here, HD)
    key_heads = keys.reshape(slot_count, heads_here, HD)
    value_heads = values.reshape(slot_count, heads_here, HD)
    grad_heads = grad_attn.reshape(slot_count, heads_here, HD)
    key_grads = jnp.zeros((slot_count, heads_here, HD), jnp.float32)
    value_grads = jnp.zeros((slot_count, heads_here, HD), jnp.float32)
    block_high = slot_count // key_span

    def key_parts(key_index):
        offset = key_index * key_span
        key_part = lax.dynamic_slice_in_dim(key_heads, offset, key_span, 0)
        value_part = lax.dynamic_slice_in_dim(value_heads, offset, key_span, 0)
        segment_part = lax.dynamic_slice_in_dim(segment, offset, key_span, 0)
        allowed = (segment[:, None] == segment_part[None, :])[None]
        return (offset, key_part, value_part, allowed)

    def max_sweep(key_index, state):
        largest, stored = state
        offset, key_part, value_part, allowed = key_parts(key_index)
        scores = (
            jnp.einsum("qhd,khd->hqk", query_heads, key_part, preferred_element_type=jnp.float32)
            * score_scale
        )
        shifted = jnp.where(allowed, scores, FLOOR_SCORE)
        largest = jnp.maximum(largest, jnp.max(shifted, axis=2))
        stored = lax.dynamic_update_slice_in_dim(stored, shifted, offset, 2)
        return (largest, stored)

    start_state = (
        jnp.full((heads_here, query_span), FLOOR_SCORE, jnp.float32),
        jnp.full((heads_here, query_span, slot_count), FLOOR_SCORE, jnp.float32),
    )
    largest, stored = lax.fori_loop(0, block_high, max_sweep, start_state)
    allowed_all = (segment[:, None] == segment[None, :])[None]
    summed = jnp.sum(jnp.where(allowed_all, jnp.exp(stored - largest[:, :, None]), 0.0), axis=2)
    positive = summed > 0.0
    safe_sum = jnp.where(positive, summed, 1.0)

    def block_probs(offset, allowed):
        shifted = lax.dynamic_slice_in_dim(stored, offset, key_span, 2)
        weights = jnp.where(allowed, jnp.exp(shifted - largest[:, :, None]), 0.0)
        return weights / safe_sum[:, :, None]

    def value_sweep(key_index, accum):
        offset, key_part, value_part, allowed = key_parts(key_index)
        probs_low = block_probs(offset, allowed).astype(jnp.bfloat16)
        return accum + jnp.einsum(
            "hqk,khd->qhd", probs_low, value_part, preferred_element_type=jnp.float32
        )

    accum = lax.fori_loop(
        0, block_high, value_sweep, jnp.zeros((query_span, heads_here, HD), jnp.float32)
    )
    attended = accum.astype(jnp.bfloat16)
    diagonal_term = jnp.sum(grad_heads.astype(jnp.float32) * attended.astype(jnp.float32), axis=2).T

    def second_sweep(key_index, state):
        grad_query, grad_key, grad_value = state
        offset, key_part, value_part, allowed = key_parts(key_index)
        probs = block_probs(offset, allowed)
        probs_low = probs.astype(jnp.bfloat16)
        grad_probs = jnp.einsum(
            "qhd,khd->hqk", grad_heads, value_part, preferred_element_type=jnp.float32
        )
        grad_scores = (probs * (grad_probs - diagonal_term[:, :, None])).astype(jnp.bfloat16)
        grad_query = grad_query + jnp.einsum(
            "hqk,khd->qhd", grad_scores, key_part, preferred_element_type=jnp.float32
        )
        key_piece = (
            jnp.einsum("hqk,qhd->khd", grad_scores, query_heads, preferred_element_type=jnp.float32)
            * score_scale
        )
        value_piece = jnp.einsum(
            "hqk,qhd->khd", probs_low, grad_heads, preferred_element_type=jnp.float32
        )
        grad_key = lax.dynamic_update_slice_in_dim(
            grad_key, lax.dynamic_slice_in_dim(grad_key, offset, key_span, 0) + key_piece, offset, 0
        )
        grad_value = lax.dynamic_update_slice_in_dim(
            grad_value,
            lax.dynamic_slice_in_dim(grad_value, offset, key_span, 0) + value_piece,
            offset,
            0,
        )
        return (grad_query, grad_key, grad_value)

    query_start = jnp.zeros((query_span, heads_here, HD), jnp.float32)
    block_query_grad, key_grads, value_grads = lax.fori_loop(
        0, block_high, second_sweep, (query_start, key_grads, value_grads)
    )
    query_grad_blocks = (block_query_grad * score_scale).astype(jnp.bfloat16)
    attended_all = attended.reshape(slot_count, local_width)
    grad_queries = query_grad_blocks.reshape(slot_count, local_width)
    grad_keys = key_grads.astype(jnp.bfloat16).reshape(slot_count, local_width)
    grad_values = value_grads.astype(jnp.bfloat16).reshape(slot_count, local_width)
    patch_total = lax.psum(filled.astype(jnp.float32), "dp")
    contract_rows = (((0,), (0,)), ((), ()))
    weight_grad = lax.psum_scatter(
        lax.dot_general(
            grad_masked, attended_all, contract_rows, preferred_element_type=jnp.float32
        ),
        "dp",
        scatter_dimension=0,
        tiled=True,
    )
    fisher_next = fisher + weight_grad * weight_grad / patch_total
    return (grad_queries, grad_keys, grad_values, weight_grad, fisher_next)


def solution(mesh):
    placed = (
        P("dp", "tensor"),
        P("dp", "tensor"),
        P("dp", "tensor"),
        P("dp", "tensor"),
        P("dp", "tensor"),
        P("dp", "tensor"),
        P("dp", None),
    )
    return jax.shard_map(
        per_device,
        mesh=mesh,
        in_specs=placed,
        out_specs=(
            P("dp", "tensor"),
            P("dp", "tensor"),
            P("dp", "tensor"),
            P("dp", "tensor"),
            P("dp", "tensor"),
        ),
        check_vma=False,
    )
```

profile of v0, /device:TPU:32, one launch (start us, length us, event | category | flops | bytes accessed | tf_op | source)
XLA Modules:
  0.0 379.8 jit_solution(6609119943611265355)
XLA Ops:
  7.2 0.7 all-gather.3.cloned.1.call-update
  7.9 0.7 all-gather.5.cloned.1.call-update
  8.7 0.8 reduce-window.4
  9.5 0.6 slice.4
  10.1 1.1 copy.40
  11.4 1.1 copy.39
  12.4 1.1 copy.43
  13.5 0.7 iota_compare_fusion.1
  14.4 1.0 while.48
  14.6 0.3 constant_dynamic-update-slice_fusion.5
  15.1 0.3 constant_dynamic-update-slice_fusion.5
  15.6 1.8 while.49
  16.0 0.5 fusion.56
  16.9 0.5 fusion.56
  17.4 25.4 %all-gather.3.cloned.1.call-done = bf16[256,6144]{1,0:T(8,128)(2,1)} async-done(((bf16[256,768]{1,0:T(8,128)(2,1)}), bf16[256,6144]{1,0:T(8,128)(2,1)}) %all-gather.3.cloned.1.call-update) | async-done | bytes 3145744 | tf_op jit(solution)/shard_map/all_gather | solution.py:25
  42.8 86.2 %all-gather.5.cloned.1.call-done = bf16[6144,384]{1,0:T(8,128)(2,1)} async-done(((bf16[192,384]{1,0:T(8,128)(2,1)}), bf16[6144,384]{1,0:T(8,128)(2,1)}) %all-gather.5.cloned.1.call-update) | async-done | bytes 4718608 | tf_op jit(solution)/shard_map/all_gather | solution.py:29
  129.0 5.1 %fusion.28 = bf16[256,384]{1,0:T(8,128)(2,1)S(1)} fusion(bf16[6144,384]{1,0:T(8,128)(2,1)} %all-gather.5.cloned.1.call-done, bf16[256,6144]{1,0:T(8,128)(2,1)} %all-gather.3.cloned.1.call-done, pred[256]{0:T(512)(128)(4,1)S(1)} %iota_compare_fusion.1), kind=kOutput, calls=%fused_computation.47 | convolution fusion | flops 1209630720 | bytes 8061184 | tf_op jit(solution)/shard_map/dot_general | solution.py:27
  134.3 7.5 %fusion.26 = f32[6144,384]{1,0:T(8,128)} fusion(bf16[256,384]{0,1:T(8,128)(2,1)S(1)} %bitcast.71, bf16[256,6144]{1,0:T(8,128)(2,1)} %all-gather.3.cloned.1.call-done, pred[256]{0:T(512)(128)(4,1)S(1)} %iota_compare_fusion.1), kind=kOutput, calls=%fused_computation.45 | convolution fusion | flops 1209532416 | bytes 12779776 | tf_op jit(solution)/shard_map/dot_general | solution.py:130
  142.5 67.0 %psum.7 = f32[]{:T(128)} all-reduce(f32[]{:T(128)S(6)} %convert_element_type.56), channel_id=1, replica_groups=mesh['dp'=32,'tensor'=8] {'dp'}, use_global_device_ids=true, to_apply=%region_12.13 | all-reduce | flops 1 | bytes 8 | tf_op jit(solution)/shard_map/psum | solution.py:127
  209.5 0.8 copy.47
  210.4 7.3 %while.50 = (s32[]{:T(128)}, f32[256,3,128]{0,2,1:T(8,128)S(1)}, f32[256,3,128]{0,2,1:T(8,128)S(1)}, f32[256,3,128]{0,2,1:T(8,128)S(1)}, bf16[256,3,128]{0,2,1:T...) while((s32[]{:T(128)}, f32[256,3,128]{0,2,1:T(8,128)S(1)}, ...), condition=%wide.region_10.11_spmd.clone, body=%wide.region_9.10_spmd.clone.sunk | while | flops 102023168 | bytes 7003893 | solution.py:119
  210.6 1.2 fusion.65
  212.0 1.2 fusion.67
  213.8 0.3 fusion.66
  214.3 1.2 fusion.65
  215.6 1.2 fusion.67
  217.4 0.3 fusion.66
  217.8 0.8 copy.53
  218.6 0.8 copy.51
  219.5 0.8 copy.52
  220.3 150.7 %reduce-scatter.2.cloned.1.call-done = f32[192,384]{1,0:T(8,128)} async-done(((f32[6144,384]{1,0:T(8,128)}), f32[192,384]{1,0:T(8,128)}) %reduce-scatter.2.cloned.1.call-update) | async-done | bytes 294928 | tf_op jit(solution)/shard_map/reduce_scatter | solution.py:129
  371.0 2.3 divide_add_fusion
  (56 shorter events, 4.1 us)
Async XLA Ops:
  7.2 35.6 %all-gather.3.cloned.1.call-start = ((), (), s32[]{:S(2)}) async-start(), calls=%async_computation.1 | async-start | bytes 3538944 | tf_op jit(solution)/shard_map/all_gather | solution.py:25
  7.9 121.1 %all-gather.5.cloned.1.call-start = ((), (), s32[]{:S(2)}) async-start(), calls=%async_computation.2 | async-start | bytes 4866048 | tf_op jit(solution)/shard_map/all_gather | solution.py:29
  8.6 362.3 %reduce-scatter.2.cloned.1.call-start = ((), (), s32[]{:S(2)}) async-start(), calls=%async_computation.3 | async-start | bytes 9732096 | tf_op jit(solution)/shard_map/reduce_scatter | solution.py:129
  217.7 153.2 %copy-start = (f32[192,384]{1,0:T(8,128)S(1)}, f32[192,384]{1,0:T(8,128)}, u32[]{:S(2)}) copy-start(f32[192,384]{1,0:T(8,128)} %param.18) | copy-start | bytes 884740
Sparse Core Ops, SparseCore 0:
  9.8 32.9 all-gather.2
  45.4 83.5 all-gather.4
  142.0 228.9 reduce-scatter.1
where the time goes:
time: 381 us; the launch traced here: 380 us
  waiting for transfers between devices  264 us (69%)
  blocking collectives  67 us (18%)
  matrix products  19.7 us (5%)
  between operations  14.5 us (4%)
  local copies, waits for them, and re-layouts  9.49 us (2%)
  other arithmetic  4.92 us (1%)
    reduce_scatter x1, waiting for transfers between devices, per_device(): lax.psum_scatter(lax.dot_general(grad_masked, attended_all, contract_rows...  151 us
    all_gather x1, waiting for transfers between devices, per_device(): lax.all_gather(out_weight, 'dp', axis=0, tiled=True)  86.2 us
    psum x1, blocking collectives, per_device(): patch_total = lax.psum(filled.astype(jnp.float32), 'dp')  67 us
    all_gather x1, waiting for transfers between devices, per_device(): whole = lax.all_gather(upstream, 'tensor', axis=1, tiled=True)  25.4 us
  transfers between devices with their start and end apart: 3, of which 3 were waited for; matrix products, arithmetic and copies ran while one was open for 5% of the time, Pallas kernels for 0%

commit v1 on v0

v1 whole, which is shorter than its diff:
```python
import functools

import jax
import jax.numpy as jnp
from jax import lax
from jax.experimental import pallas as pl
from jax.experimental.pallas import tpu as pltpu
from jax.sharding import PartitionSpec as P

MESH = pl.DeviceIdType.MESH
HD = 128
NX, NY, NZ = 4, 4, 8
FLOOR_SCORE = -1e30
F32, BF16 = jnp.float32, jnp.bfloat16
N_REMOTE = 96
N_LOCAL = 16

NN = (((1,), (0,)), ((), ()))
NT = (((1,), (1,)), ((), ()))
TN = (((0,), (0,)), ((), ()))


def dot(a, b, dims):
    return lax.dot_general(a, b, dims, preferred_element_type=F32)


def kernel(
    len_ref, q_hbm, k_hbm, v_hbm, up_hbm, w_hbm, fisher_hbm,
    gq_hbm, gk_hbm, gv_hbm, wg_hbm, fn_hbm,
    q_v, k_v, v_v, up_v, fisher_v, gq_v, gk_v, gv_v, wg_v, fn_v,
    up_t, g_all, g_relay, w_all, w_t, att_t, probs_t,
    xs_far, xr_far, xs_sum, xr_sum, x_acc, grad_t,
    zs, zr, z_acc, cnt, cnt_x, cnt_z,
    send_sem, recv_sem, local_sem,
):
    tokens = up_v.shape[0]
    rows = w_hbm.shape[0]
    half = rows // 2
    width = q_v.shape[1]
    heads = width // HD
    scale = HD ** (-0.5)

    dp, tau = lax.axis_index("dp"), lax.axis_index("tensor")
    z, x = dp // NX, dp % NX
    y, c = tau // 2, tau % 2

    def at(dz=0, dx=0, dy=0, other=False):
        pz, px, py = (z + dz + NZ) % NZ, (x + dx + NX) % NX, (y + dy + NY) % NY
        return (pz * NX + px, py * 2 + (1 - c if other else c))

    def block(index, start=0, size=rows):
        return pl.ds(pl.multiple_of(index * rows + start, 16), size)

    sent = []
    index_of = {}

    def message(name, src, dst, to):
        number = index_of.setdefault(name, len(index_of))
        return pltpu.make_async_remote_copy(
            src_ref=src, dst_ref=dst, send_sem=send_sem.at[number], recv_sem=recv_sem.at[number],
            device_id=to, device_id_type=MESH,
        )

    pending = {}

    def send(name, src, dst, to):
        copy = message(name, src, dst, to)
        copy.start()
        pending[name] = copy
        sent.append(copy)

    def arrive(name):
        pending[name].wait_recv()

    locals_ = {}

    def load(name, src, dst):
        copy = pltpu.make_async_copy(src, dst, local_sem.at[len(locals_)])
        copy.start()
        locals_[name] = copy

    load("up", up_hbm, up_v)
    load("q", q_hbm, q_v)
    load("k", k_hbm, k_v)
    load("v", v_hbm, v_v)
    load("w", w_hbm, w_all.at[block(z)])
    load("fisher", fisher_hbm, fisher_v)

    peers = [at(dz=d) for d in range(1, NZ)] + [at(dx=d) for d in range(1, NX)]
    peers += [at(dy=1), at(dy=-1), at(other=True)]
    barrier = pltpu.get_barrier_semaphore()
    for peer in peers:
        pl.semaphore_signal(barrier, inc=1, device_id=peer, device_id_type=MESH)

    finish = []
    total = jnp.int32(0)
    for j in range(len_ref.shape[1]):
        total = total + len_ref[0, j]
        finish.append(total)
    filled = finish[-1]
    cnt[...] = jnp.full(cnt.shape, filled.astype(F32), F32)

    locals_["up"].wait()
    with jax.named_scope("transpose_upstream"):
        inside = lax.broadcasted_iota(jnp.int32, (tokens, HD), 0) < filled
        for j in range(up_v.shape[1] // HD):
            piece = up_v[:, j * HD:(j + 1) * HD].astype(F32)
            up_t[j * HD:(j + 1) * HD, :] = jnp.where(inside, piece, 0.0).T.astype(BF16)
        g_all[0, block(tau), :] = up_t[block(x), :]

    with jax.named_scope("entry_barrier"):
        pl.semaphore_wait(barrier, len(peers))

    A, B = pl.ds(0, half), pl.ds(half, half)

    def w_rows(index, part):
        return w_all.at[block(index, 0 if part == "A" else half, half)]

    for part, cut in (("A", A), ("B", B)):
        send(f"w+1{part}", w_hbm.at[cut], w_rows(z, part), at(dz=1))
    for part, cut in (("B", B), ("A", A)):
        send(f"w-1{part}", w_hbm.at[cut], w_rows(z, part), at(dz=-1))
    x_next, x_prev, x_far = (x + 1) % NX, (x + NX - 1) % NX, (x + 2) % NX
    send("g2A", up_t.at[block(x_far, 0, half)], g_relay.at[0], at(dx=1))
    send("g2B", up_t.at[block(x_far, half, half)], g_relay.at[1], at(dx=-1))
    send("g1+", up_t.at[block(x_next)], g_all.at[3, block(tau)], at(dx=1))
    send("g1-", up_t.at[block(x_prev)], g_all.at[1, block(tau)], at(dx=-1))
    for d in range(1, NX):
        send(f"cx{d}", cnt, cnt_x.at[d], at(dx=d))

    def spread(slot):
        piece = g_all.at[slot, block(tau)]
        send(f"y{slot}+", piece, piece, at(dy=1))
        send(f"y{slot}-", piece, piece, at(dy=-1))
        send(f"s{slot}0", piece, piece, at(other=True))

    def y_rows(dy, part=None):
        row = ((y + dy + NY) % NY) * 2 + c
        if part is None:
            return block(row)
        return block(row, 0 if part == "A" else half, half)

    def relay_y(slot):
        arrive(f"y{slot}+")
        piece = g_all.at[slot, y_rows(-1, "A")]
        send(f"y{slot}A", piece, piece, at(dy=1))
        piece = g_all.at[slot, y_rows(-1)]
        send(f"s{slot}1", piece, piece, at(other=True))
        arrive(f"y{slot}-")
        piece = g_all.at[slot, y_rows(1, "B")]
        send(f"y{slot}B", piece, piece, at(dy=-1))
        piece = g_all.at[slot, y_rows(1)]
        send(f"s{slot}2", piece, piece, at(other=True))

    def end_y(slot):
        arrive(f"y{slot}A")
        arrive(f"y{slot}B")
        piece = g_all.at[slot, y_rows(2)]
        send(f"s{slot}3", piece, piece, at(other=True))

    def end_core(slot):
        for j in range(4):
            arrive(f"s{slot}{j}")

    def relay_w(step, part, directions="+-"):
        for sign in directions:
            arrive(f"w{sign}{step - 1}{part}")
            one = 1 if sign == "+" else -1
            source = (z - one * (step - 1) + NZ) % NZ
            send(f"w{sign}{step}{part}", w_rows(source, part), w_rows(source, part), at(dz=one))

    spread(0)

    u_position = lax.broadcasted_iota(jnp.int32, (tokens, 1), 0)
    t_position = lax.broadcasted_iota(jnp.int32, (1, tokens), 1)
    u_segment = jnp.zeros((tokens, 1), jnp.int32)
    t_segment = jnp.zeros((1, tokens), jnp.int32)
    for end in finish:
        u_segment += (u_position >= end).astype(jnp.int32)
        t_segment += (t_position >= end).astype(jnp.int32)

    def forward(h):
        span = pl.ds(h * HD, HD)
        scores = dot(k_v[:, span], q_v[:, span], NT) * scale
        shifted = jnp.where(u_segment == t_segment, scores, FLOOR_SCORE)
        largest = jnp.max(shifted, axis=0, keepdims=True)
        weights = jnp.exp(shifted - largest)
        probs = weights * (1.0 / jnp.sum(weights, axis=0, keepdims=True))
        probs_t[h] = probs
        att_t[0, span, :] = dot(v_v[:, span], probs.astype(BF16), TN).astype(BF16)

    for name in ("q", "k", "v"):
        locals_[name].wait()
    with jax.named_scope("forward0"):
        forward(0)
    with jax.named_scope("relay_g"):
        arrive("g2A")
        send("g2a", g_relay.at[0], g_all.at[2, block(tau, 0, half)], at(dx=1))
        arrive("g2B")
        send("g2b", g_relay.at[1], g_all.at[2, block(tau, half, half)], at(dx=-1))
    with jax.named_scope("forward1"):
        forward(1)
    with jax.named_scope("relay_w2A"):
        relay_w(2, "A", "+")
        relay_w(2, "B", "-")
    with jax.named_scope("forward2"):
        forward(2)
    send("a+", att_t.at[0], att_t.at[3], at(dx=1))
    send("a-", att_t.at[0], att_t.at[1], at(dx=-1))

    with jax.named_scope("relay_w2B"):
        relay_w(2, "B", "+")
        relay_w(2, "A", "-")
    with jax.named_scope("relay_y0"):
        relay_y(0)
    with jax.named_scope("spread2"):
        arrive("g2a")
        arrive("g2b")
        spread(2)
    with jax.named_scope("spread13"):
        arrive("g1+")
        spread(3)
        arrive("g1-")
        spread(1)
    with jax.named_scope("counts"):
        for d in range(1, NX):
            arrive(f"cx{d}")
        cnt_z[0] = cnt[...] + cnt_x[1] + cnt_x[2] + cnt_x[3]
        for d in range(1, NZ):
            send(f"cz{d}", cnt_z.at[0], cnt_z.at[d], at(dz=d))
    with jax.named_scope("relay_w3A"):
        relay_w(3, "A", "+")
        relay_w(3, "B", "-")
    with jax.named_scope("relay_w3B"):
        relay_w(3, "B", "+")
        relay_w(3, "A", "-")
    with jax.named_scope("relay_a"):
        arrive("a+")
        send("aA", att_t.at[3, pl.ds(0, width // 2)], att_t.at[2, pl.ds(0, width // 2)], at(dx=1))
        arrive("a-")
        send("aB", att_t.at[1, pl.ds(width // 2, width // 2)], att_t.at[2, pl.ds(width // 2, width // 2)], at(dx=-1))
    with jax.named_scope("relay_w4"):
        relay_w(4, "A", "+")
        relay_w(4, "B", "-")
    with jax.named_scope("relay_y2"):
        end_y(0)
        relay_y(2)
    with jax.named_scope("relay_y13"):
        relay_y(3)
        relay_y(1)
        end_y(2)
    with jax.named_scope("end_w"):
        arrive("w+3B")
        arrive("w-3A")
        arrive("w+4A")
        arrive("w-4B")
        locals_["w"].wait()
        for j in range(w_all.shape[0] // HD):
            w_t[:, j * HD:(j + 1) * HD] = w_all[j * HD:(j + 1) * HD, :].T

    def grad_part(slot):
        return dot(w_t[...], g_all[slot], NN)

    def weight_part(offset, slot):
        target = (z + offset + NZ) % NZ
        for j in range(NX):
            term = dot(g_all[j, block(target), :], att_t[j], NT)
            if j == 0:
                z_acc[slot] = term
            else:
                z_acc[slot] += term

    x_half = width // 2
    XA, XB = pl.ds(0, x_half), pl.ds(x_half, x_half)
    with jax.named_scope("part_x_far"):
        end_core(2)
        xs_far[...] = grad_part(2).astype(BF16)
        send("rA", xs_far.at[XA], xr_far.at[0], at(dx=1))
        send("rB", xs_far.at[XB], xr_far.at[1], at(dx=-1))
    with jax.named_scope("end_y13"):
        end_y(3)
        end_y(1)
        end_core(0)
        end_core(3)
        x_acc[1] = grad_part(3)
        end_core(1)
        x_acc[0] = grad_part(1)
    with jax.named_scope("end_a"):
        arrive("aA")
        arrive("aB")

    halves = {"A": A, "B": B}
    slot_of = {}

    def send_z(sign, step, part, slot):
        cut = halves[part]
        value = z_acc[slot, cut, :]
        before = (sign, step - 1, part)
        if before in slot_of:
            arrive(f"z{sign}{step - 1}{part}")
            value = value + zr[slot_of[before]].astype(F32)
        mine = slot_of.setdefault((sign, step, part), len(slot_of))
        zs[mine] = value.astype(BF16)
        send(f"z{sign}{step}{part}", zs.at[mine], zr.at[mine], at(dz=1 if sign == "+" else -1))

    with jax.named_scope("part_z4"):
        weight_part(4, 0)
        send_z("+", 1, "A", 0)
        send_z("-", 1, "B", 0)
    with jax.named_scope("sum_x1"):
        arrive("rA")
        x_acc[0, XA, :] += xr_far[0].astype(F32)
        xs_sum[0] = x_acc[0].astype(BF16)
        send("r+", xs_sum.at[0], xr_sum.at[0], at(dx=1))
        arrive("rB")
        x_acc[1, XB, :] += xr_far[1].astype(F32)
        xs_sum[1] = x_acc[1].astype(BF16)
        send("r-", xs_sum.at[1], xr_sum.at[1], at(dx=-1))
    with jax.named_scope("part_z3"):
        weight_part(3, 0)
        send_z("+", 2, "B", 0)
        weight_part(-3, 1)
        send_z("-", 2, "A", 1)
        send_z("+", 2, "A", 0)
        send_z("-", 2, "B", 1)
    with jax.named_scope("part_z2"):
        weight_part(2, 0)
        weight_part(-2, 1)
        send_z("+", 3, "B", 0)
        send_z("-", 3, "A", 1)
        send_z("+", 3, "A", 0)
        send_z("-", 3, "B", 1)
    with jax.named_scope("part_x0"):
        x_acc[0] = grad_part(0)
    with jax.named_scope("part_z1"):
        weight_part(1, 0)
        weight_part(-1, 1)
        send_z("+", 4, "B", 0)
        send_z("-", 4, "A", 1)
        send_z("+", 4, "A", 0)
        send_z("-", 4, "B", 1)
    with jax.named_scope("end_x"):
        arrive("r+")
        arrive("r-")
        grad_t[...] = (x_acc[0] + xr_sum[0].astype(F32) + xr_sum[1].astype(F32)).astype(BF16)

    def backward(h):
        span = pl.ds(h * HD, HD)
        probs = probs_t[h]
        out_grad = grad_t[span, :]
        diagonal = jnp.sum(out_grad.astype(F32) * att_t[0, span, :].astype(F32), axis=0, keepdims=True)
        grad_probs = dot(v_v[:, span], out_grad, NN)
        grad_scores = (probs * (grad_probs - diagonal)).astype(BF16)
        gk_v[:, span] = (dot(grad_scores, q_v[:, span], NN) * scale).astype(BF16)
        gq_v[:, span] = (dot(grad_scores, k_v[:, span], TN) * scale).astype(BF16)
        gv_v[:, span] = dot(probs.astype(BF16), out_grad, NT).astype(BF16)

    with jax.named_scope("backward"):
        for h in range(heads):
            backward(h)
    load("gq", gq_v, gq_hbm)
    load("gk", gk_v, gk_hbm)
    load("gv", gv_v, gv_hbm)

    with jax.named_scope("part_z0"):
        weight_part(0, 0)
        for d in range(1, NZ):
            arrive(f"cz{d}")
        patches = cnt_z[0]
        for d in range(1, NZ):
            patches = patches + cnt_z[d]
        inverse = 1.0 / patches[0:1, 0:1]
        locals_["fisher"].wait()
    with jax.named_scope("end_z"):
        for part in ("B", "A"):
            cut = halves[part]
            value = z_acc[0, cut, :]
            for sign in "+-":
                arrive(f"z{sign}4{part}")
                value = value + zr[slot_of[(sign, 4, part)]].astype(F32)
            wg_v[cut, :] = value
            fn_v[cut, :] = fisher_v[cut, :] + value * value * inverse
    load("wg", wg_v, wg_hbm)
    load("fn", fn_v, fn_hbm)

    with jax.named_scope("drain"):
        for copy in sent:
            copy.wait_send()
        for name in ("gq", "gk", "gv", "wg", "fn"):
            locals_[name].wait()


def per_device(queries, keys, values, upstream, out_weight, fisher, image_lengths):
    tokens, width = queries.shape
    rows = out_weight.shape[0]
    half = rows // 2
    heads = width // HD
    hbm = pl.BlockSpec(memory_space=pl.ANY)
    vm = pltpu.VMEM
    scratch = [
        vm((tokens, width), BF16),
        vm((tokens, width), BF16),
        vm((tokens, width), BF16),
        vm(upstream.shape, BF16),
        vm((rows, width), F32),
        vm((tokens, width), BF16),
        vm((tokens, width), BF16),
        vm((tokens, width), BF16),
        vm((rows, width), F32),
        vm((rows, width), F32),
        vm((upstream.shape[1], tokens), BF16),
        vm((NX, NZ * rows, tokens), BF16),
        vm((2, half, tokens), BF16),
        vm((NZ * rows, width), BF16),
        vm((width, NZ * rows), BF16),
        vm((NX, width, tokens), BF16),
        vm((heads, tokens, tokens), F32),
        vm((width, tokens), BF16),
        vm((2, width // 2, tokens), BF16),
        vm((2, width, tokens), BF16),
        vm((2, width, tokens), BF16),
        vm((2, width, tokens), F32),
        vm((width, tokens), BF16),
        vm((14, half, width), BF16),
        vm((14, half, width), BF16),
        vm((2, rows, width), F32),
        vm((8, HD), F32),
        vm((NX, 8, HD), F32),
        vm((NZ, 8, HD), F32),
        pltpu.SemaphoreType.DMA((N_REMOTE,)),
        pltpu.SemaphoreType.DMA((N_REMOTE,)),
        pltpu.SemaphoreType.DMA((N_LOCAL,)),
    ]
    return pl.pallas_call(
        kernel,
        out_shape=[
            jax.ShapeDtypeStruct((tokens, width), BF16),
            jax.ShapeDtypeStruct((tokens, width), BF16),
            jax.ShapeDtypeStruct((tokens, width), BF16),
            jax.ShapeDtypeStruct((rows, width), F32),
            jax.ShapeDtypeStruct((rows, width), F32),
        ],
        in_specs=[pl.BlockSpec(memory_space=pltpu.SMEM)] + [hbm] * 6,
        out_specs=[hbm] * 5,
        scratch_shapes=scratch,
        compiler_params=pltpu.CompilerParams(
            collective_id=0, has_side_effects=True, vmem_limit_bytes=40 * 1024 * 1024
        ),
    )(image_lengths, queries, keys, values, upstream, out_weight, fisher)


def solution(mesh):
    placed = P("dp", "tensor")
    return jax.shard_map(
        per_device,
        mesh=mesh,
        in_specs=(placed,) * 6 + (P("dp", None),),
        out_specs=(placed,) * 5,
        check_vma=False,
    )
```

time: 381 us -> 62.1 us (0.16)
  waiting for transfers between devices: 264 us -> 0 us
  blocking collectives: 67 us -> 0 us
  Pallas kernels: 0 us -> 51.4 us
  matrix products: 19.7 us -> 0 us
  between operations: 14.5 us -> 0.66 us
  other arithmetic: 4.92 us -> 0 us
    reduce_scatter x1 -> x0, waiting for transfers between devices: 151 us -> none  [per_device(): lax.psum_scatter(lax.dot_general(grad_masked, attended_all, contract_rows...]
    all_gather x2 -> x0, waiting for transfers between devices: 112 us -> none  [the longest x1 86.2 us: per_device(): lax.all_gather(out_weight, 'dp', axis=0, tiled=True)]
    psum x1 -> x0, blocking collectives: 67 us -> none  [per_device(): patch_total = lax.psum(filled.astype(jnp.float32), 'dp')]
    pallas_call x0 -> x1, Pallas kernels: none -> 51.4 us  [per_device(): pl.pallas_call(kernel, out_shape=[jax.ShapeDtypeStruct((tokens, width), B...]
    dot_general x14 -> x0, matrix products: 19.7 us -> none  [the longest x1 7.48 us: per_device(): lax.dot_general(grad_masked, attended_all, contract_rows, preferred_eleme...]
    unnamed x10 -> x19, local copies, waits for them, and re-layouts: 6.62 us -> 9.75 us
  transfers between devices with their start and end apart: 3 -> 0, of which waited for: 3 -> 0; matrix products, arithmetic and copies ran while one was open for 5% -> 0% of each run, Pallas kernels for 0% -> 0%
where the time goes in v1:
time: 62.1 us; the launch traced here: 61.9 us
  Pallas kernels  51.4 us (83%)
  local copies, waits for them, and re-layouts  9.75 us (16%)
  between operations  0.66 us (1%)
    pallas_call x1, Pallas kernels, per_device(): pl.pallas_call(kernel, out_shape=[jax.ShapeDtypeStruct((tokens, width), B...  51.4 us
    unnamed x19, local copies, waits for them, and re-layouts  9.75 us

profile of v1, /device:TPU:32, one launch (start us, length us, event | category | flops | bytes accessed | tf_op | source)
XLA Modules:
  0.0 61.9 jit_solution(2085842566775474822)
XLA Ops:
  0.6 0.0 copy-start
  0.6 1.0 %copy-done = bf16[256,768]{1,0:T(8,128)(2,1)S(1)} copy-done((bf16[256,768]{1,0:T(8,128)(2,1)S(1)}, bf16[256,768]{1,0:T(8,128)(2,1)}, u32[]{:S(2)}) %copy-start) | copy-done | bytes 393240
  1.6 0.0 copy-start.1
  1.6 1.0 %copy-done.1 = f32[192,384]{1,0:T(8,128)S(1)} copy-done((f32[192,384]{1,0:T(8,128)S(1)}, f32[192,384]{1,0:T(8,128)}, u32[]{:S(2)}) %copy-start.1) | copy-done | bytes 294936
  2.6 0.0 copy-start.2
  2.6 0.9 %copy-done.2 = bf16[256,384]{1,0:T(8,128)(2,1)S(1)} copy-done((bf16[256,384]{1,0:T(8,128)(2,1)S(1)}, bf16[256,384]{1,0:T(8,128)(2,1)}, u32[]{:S(2)}) %copy-start.2) | copy-done | bytes 196632
  3.5 0.0 copy-start.3
  3.5 0.9 %copy-done.3 = bf16[256,384]{1,0:T(8,128)(2,1)S(1)} copy-done((bf16[256,384]{1,0:T(8,128)(2,1)S(1)}, bf16[256,384]{1,0:T(8,128)(2,1)}, u32[]{:S(2)}) %copy-start.3) | copy-done | bytes 196632
  4.4 0.0 copy-start.4
  4.4 0.9 %copy-done.4 = bf16[256,384]{1,0:T(8,128)(2,1)S(1)} copy-done((bf16[256,384]{1,0:T(8,128)(2,1)S(1)}, bf16[256,384]{1,0:T(8,128)(2,1)}, u32[]{:S(2)}) %copy-start.4) | copy-done | bytes 196632
  5.4 0.0 copy-start.5
  5.4 0.9 %copy-done.5 = bf16[192,384]{1,0:T(8,128)(2,1)S(1)} copy-done((bf16[192,384]{1,0:T(8,128)(2,1)S(1)}, bf16[192,384]{1,0:T(8,128)(2,1)}, u32[]{:S(2)}) %copy-start.5) | copy-done | bytes 147480
  6.3 0.0 copy-start.6
  6.3 0.7 %copy-done.6 = s32[1,8]{1,0:T(1,128)S(1)} copy-done((s32[1,8]{1,0:T(1,128)S(1)}, s32[1,8]{1,0:T(1,128)}, u32[]{:S(2)}) %copy-start.6) | copy-done | bytes 56
  6.9 51.4 %shard_map.110 = (bf16[256,384]{1,0:T(8,128)(2,1)S(1)}, bf16[256,384]{1,0:T(8,128)(2,1)S(1)}, bf16[256,384]{1,0:T(8,128)(2,1)S(1)}, f32[192,384]{1,0:T(8,128)S(1)}, f32[192,384]{1,0:T(8,128)S(1)}) custom-call(s32[1,8]{1,0:T(1,128)S(1)} %copy-done.6, bf16[256,384]{1,0:T(8,128)(2,1)S(1)} %copy-done.2, bf16[256,384]{1,0:T(8,128)(2,1)S(1)} %copy-done.3, ...), custom_call_target="tpu_custom_call" | custom-call | tf_op jit(solution)/shard_map/pallas_call | solution.py:434
  58.4 0.7 %copy.17 = bf16[256,384]{1,0:T(8,128)(2,1)} copy(bf16[256,384]{1,0:T(8,128)(2,1)S(1)} %get-tuple-element.10) | data formatting | bytes 393216
  59.1 0.7 %copy.18 = bf16[256,384]{1,0:T(8,128)(2,1)} copy(bf16[256,384]{1,0:T(8,128)(2,1)S(1)} %get-tuple-element.11) | data formatting | bytes 393216
  59.8 0.7 %copy.19 = bf16[256,384]{1,0:T(8,128)(2,1)} copy(bf16[256,384]{1,0:T(8,128)(2,1)S(1)} %get-tuple-element.12) | data formatting | bytes 393216
  60.4 0.7 %copy.20 = f32[192,384]{1,0:T(8,128)} copy(f32[192,384]{1,0:T(8,128)S(1)} %get-tuple-element.13) | data formatting | bytes 589824
  61.1 0.7 %copy.21 = f32[192,384]{1,0:T(8,128)} copy(f32[192,384]{1,0:T(8,128)S(1)} %get-tuple-element.14) | data formatting | bytes 589824
Async XLA Ops:
  0.6 1.0 %copy-start = (bf16[256,768]{1,0:T(8,128)(2,1)S(1)}, bf16[256,768]{1,0:T(8,128)(2,1)}, u32[]{:S(2)}) copy-start(bf16[256,768]{1,0:T(8,128)(2,1)} %up_hbm.1) | copy-start | bytes 1179652
  1.6 1.0 %copy-start.1 = (f32[192,384]{1,0:T(8,128)S(1)}, f32[192,384]{1,0:T(8,128)}, u32[]{:S(2)}) copy-start(f32[192,384]{1,0:T(8,128)} %fisher_hbm.1) | copy-start | bytes 884740
  2.6 0.9 %copy-start.2 = (bf16[256,384]{1,0:T(8,128)(2,1)S(1)}, bf16[256,384]{1,0:T(8,128)(2,1)}, u32[]{:S(2)}) copy-start(bf16[256,384]{1,0:T(8,128)(2,1)} %q_hbm.1) | copy-start | bytes 589828
  3.5 0.9 %copy-start.3 = (bf16[256,384]{1,0:T(8,128)(2,1)S(1)}, bf16[256,384]{1,0:T(8,128)(2,1)}, u32[]{:S(2)}) copy-start(bf16[256,384]{1,0:T(8,128)(2,1)} %k_hbm.1) | copy-start | bytes 589828
  4.4 0.9 %copy-start.4 = (bf16[256,384]{1,0:T(8,128)(2,1)S(1)}, bf16[256,384]{1,0:T(8,128)(2,1)}, u32[]{:S(2)}) copy-start(bf16[256,384]{1,0:T(8,128)(2,1)} %v_hbm.1) | copy-start | bytes 589828
  5.4 0.9 %copy-start.5 = (bf16[192,384]{1,0:T(8,128)(2,1)S(1)}, bf16[192,384]{1,0:T(8,128)(2,1)}, u32[]{:S(2)}) copy-start(bf16[192,384]{1,0:T(8,128)(2,1)} %w_hbm.1) | copy-start | bytes 442372
  6.3 0.7 %copy-start.6 = (s32[1,8]{1,0:T(1,128)S(1)}, s32[1,8]{1,0:T(1,128)}, u32[]{:S(2)}) copy-start(s32[1,8]{1,0:T(1,128)} %len_ref.1) | copy-start | bytes 100

commit v2 on v0

v2 whole, which is shorter than its diff:
```python
import functools

import jax
import jax.numpy as jnp
from jax import lax
from jax.experimental import pallas as pl
from jax.experimental.pallas import tpu as pltpu
from jax.sharding import PartitionSpec as P

MESH = pl.DeviceIdType.MESH
HD = 128
NX, NY, NZ = 4, 4, 8
FLOOR_SCORE = -1e30
F32, BF16 = jnp.float32, jnp.bfloat16
N_REMOTE = 128
N_LOCAL = 16
VMEM_LIMIT = 48 * 1024 * 1024

ORDER = (
    "start", "fwd0", "fwd1", "fwd2", "at", "spread30", "ry0+0", "ry0-0", "spread10", "rw+2A", "rw-2B",
    "spread31", "ry0+1", "ry0-1", "spread11", "rw+2B", "rw-2A", "spread20", "ry3+0", "ry3-0", "spread21",
    "rw+3A", "rw-3B", "ey00", "ry1-0", "ry1+0", "ry3-1", "rw+3B", "rw-3A", "ry3+1", "ey01", "ry1+1", "ry1-1",
    "rw+4A", "rw-4B", "counts", "ry2+0", "ry2-0", "ey30", "ry2-1", "ry2+1", "ey31", "wt", "ey10", "ey11",
    "px3", "ey20", "ey21", "px1", "px2", "px0", "pz4", "sz+1A0", "sz+1A1", "sz-1B0", "sz-1B1", "pz3",
    "sz+2B0", "sz+2B1", "pz-3", "sz-2A0", "sz-2A1", "pz2", "pz-2", "pz1", "pz-1", "pz0", "sz+2A0", "sz-2B0",
    "sz+2A1", "sz-2B1", "sz+3B0", "sz-3A0", "sz+3B1", "sz-3A1", "sz+3A0", "sz-3B0", "sz+3A1", "sz-3B1",
    "sz+4B0", "sz-4A0", "sz+4B1", "sz-4A1", "sz+4A0", "sz-4B0", "sz+4A1", "sz-4B1", "bwd", "end",
)

NN = (((1,), (0,)), ((), ()))
NT = (((1,), (1,)), ((), ()))
TN = (((0,), (0,)), ((), ()))


def dot(a, b, dims):
    return lax.dot_general(a, b, dims, preferred_element_type=F32)


def kernel(
    len_hbm, q_hbm, k_hbm, v_hbm, up_hbm, w_hbm, fisher_hbm,
    gq_v, gk_v, gv_v, wg_v, fn_v,
    q_v, k_v, v_v, up_v, fisher_v,
    up_t, g_all, w_all, w_t, att_t, probs_t,
    xs, xr, x_own, grad_t,
    zs, zr, z_acc, cnt, cnt_x, cnt_z, len_ref,
    send_sem, recv_sem, local_sem,
):
    tokens = up_v.shape[0]
    rows = w_hbm.shape[0]
    half = rows // 2
    width = q_v.shape[1]
    heads = width // HD
    scale = HD ** (-0.5)

    dp, tau = lax.axis_index("dp"), lax.axis_index("tensor")
    z, x = dp // NX, dp % NX
    y, c = tau // 2, tau % 2

    def at(dz=0, dx=0, dy=0, other=False):
        pz, px, py = (z + dz + NZ) % NZ, (x + dx + NX) % NX, (y + dy + NY) % NY
        return (pz * NX + px, py * 2 + (1 - c if other else c))

    def block(index, start=0, size=rows):
        return pl.ds(pl.multiple_of(index * rows + start, 16), size)

    pending = {}

    def send(name, src, dst, to):
        number = len(pending)
        copy = pltpu.make_async_remote_copy(
            src_ref=src, dst_ref=dst, send_sem=send_sem.at[number], recv_sem=recv_sem.at[number],
            device_id=to, device_id_type=MESH,
        )
        copy.start()
        pending[name] = copy

    def arrive(*names):
        for name in names:
            pending[name].wait_recv()

    locals_ = {}

    def load(name, src, dst):
        copy = pltpu.make_async_copy(src, dst, local_sem.at[len(locals_)])
        copy.start()
        locals_[name] = copy

    load("len", len_hbm, len_ref)
    load("up", up_hbm, up_v)
    load("q", q_hbm, q_v)
    load("k", k_hbm, k_v)
    load("v", v_hbm, v_v)
    load("w", w_hbm, w_all.at[block(z)])
    load("fisher", fisher_hbm, fisher_v)

    peers = [at(dz=d) for d in range(1, NZ)] + [at(dx=d) for d in range(1, NX)]
    peers += [at(dy=1), at(dy=-1), at(other=True)]
    barrier = pltpu.get_barrier_semaphore()
    for peer in peers:
        pl.semaphore_signal(barrier, inc=1, device_id=peer, device_id_type=MESH)

    locals_["len"].wait()
    finish = []
    total = jnp.int32(0)
    for j in range(len_ref.shape[1]):
        total = total + len_ref[0, j]
        finish.append(total)
    filled = finish[-1]
    cnt[...] = jnp.full(cnt.shape, filled.astype(F32), F32)

    u_position = lax.broadcasted_iota(jnp.int32, (tokens, 1), 0)
    t_position = lax.broadcasted_iota(jnp.int32, (1, tokens), 1)
    u_segment = jnp.zeros((tokens, 1), jnp.int32)
    t_segment = jnp.zeros((1, tokens), jnp.int32)
    for end in finish:
        u_segment += (u_position >= end).astype(jnp.int32)
        t_segment += (t_position >= end).astype(jnp.int32)

    locals_["up"].wait()
    inside = lax.broadcasted_iota(jnp.int32, (tokens, HD), 0) < filled
    for j in range(up_v.shape[1] // HD):
        piece = up_v[:, j * HD:(j + 1) * HD].astype(F32)
        up_t[j * HD:(j + 1) * HD, :] = jnp.where(inside, piece, 0.0).T.astype(BF16)
    g_all[0, block(tau), :] = up_t[block(x), :]
    pl.semaphore_wait(barrier, len(peers))

    def w_rows(index, part):
        return w_all.at[block(index, 0 if part == "A" else half, half)]

    def relay_w(sign, step, part):
        arrive(f"w{sign}{step - 1}{part}")
        one = 1 if sign == "+" else -1
        rows_there = w_rows((z - one * (step - 1) + NZ) % NZ, part)
        send(f"w{sign}{step}{part}", rows_there, rows_there, at(dz=one))

    def g_rows(slot, dy, part):
        return g_all.at[slot, block(((y + dy + NY) % NY) * 2 + c, part * half, half)]

    def spread(slot, part):
        if slot:
            arrive(f"g{slot}{part}")
        piece = g_rows(slot, 0, part)
        send(f"y{slot}+{part}", piece, piece, at(dy=1))
        send(f"y{slot}-{part}", piece, piece, at(dy=-1))
        send(f"s{slot}0{part}", piece, piece, at(other=True))

    def relay_y(slot, sign, part):
        arrive(f"y{slot}{sign}{part}")
        one = 1 if sign == "+" else -1
        piece = g_rows(slot, -one, part)
        if (part == 0) == (sign == "+"):
            send(f"y{slot}{sign}{part}F", piece, piece, at(dy=one))
        send(f"s{slot}{sign}{part}", piece, piece, at(other=True))

    def end_y(slot, part):
        arrive(f"y{slot}{'+' if part == 0 else '-'}{part}F")
        piece = g_rows(slot, 2, part)
        send(f"s{slot}3{part}", piece, piece, at(other=True))

    def end_core(slot):
        for j in "0+-3":
            for part in (0, 1):
                arrive(f"s{slot}{j}{part}")

    def start():
        for part, cut in (("A", pl.ds(0, half)), ("B", pl.ds(half, half))):
            send(f"w+1{part}", w_hbm.at[cut], w_rows(z, part), at(dz=1))
        for part, cut in (("B", pl.ds(half, half)), ("A", pl.ds(0, half))):
            send(f"w-1{part}", w_hbm.at[cut], w_rows(z, part), at(dz=-1))
        for part in (0, 1):
            for slot, dx in ((3, 1), (1, -1)):
                there = (x + dx + NX) % NX
                send(f"g{slot}{part}", up_t.at[block(there, part * half, half)], g_rows(slot, 0, part), at(dx=dx))
            spread(0, part)
        for part in (0, 1):
            there = (x + 2) % NX
            send(f"g2{part}", up_t.at[block(there, part * half, half)], g_rows(2, 0, part), at(dx=2))
        for d in range(1, NX):
            send(f"cx{d}", cnt, cnt_x.at[d], at(dx=d))
        for name in ("q", "k", "v"):
            locals_[name].wait()

    def forward(h):
        span = pl.ds(h * HD, HD)
        scores = dot(k_v[:, span], q_v[:, span], NT) * scale
        shifted = jnp.where(u_segment == t_segment, scores, FLOOR_SCORE)
        largest = jnp.max(shifted, axis=0, keepdims=True)
        weights = jnp.exp(shifted - largest)
        probs = weights * (1.0 / jnp.sum(weights, axis=0, keepdims=True))
        probs_t[h] = probs
        att_t[0, span, :] = dot(v_v[:, span], probs.astype(BF16), TN).astype(BF16)

    def share_attended():
        for d in (1, 3, 2):
            send(f"a{d}", att_t.at[0], att_t.at[(NX - d) % NX], at(dx=d))

    def counts():
        arrive(*(f"cx{d}" for d in range(1, NX)))
        cnt_z[0] = cnt[...] + cnt_x[1] + cnt_x[2] + cnt_x[3]
        for d in range(1, NZ):
            send(f"cz{d}", cnt_z.at[0], cnt_z.at[d], at(dz=d))

    def end_w():
        arrive("w+3B", "w-3A", "w+4A", "w-4B")
        locals_["w"].wait()
        for j in range(w_all.shape[0] // HD):
            w_t[:, j * HD:(j + 1) * HD] = w_all[j * HD:(j + 1) * HD, :].T

    def grad_part(slot):
        end_core(slot)
        term = dot(w_t[...], g_all[slot], NN)
        if slot == 0:
            x_own[...] = term
        else:
            xs[slot] = term.astype(BF16)
            send(f"r{slot}", xs.at[slot], xr.at[slot], at(dx=slot))

    def weight_part(offset):
        if offset == 4:
            arrive("a1", "a2", "a3")
        target = (z + offset + NZ) % NZ
        z_acc[offset % NZ] = sum(dot(g_all[j, block(target), :], att_t[j], NT) for j in range(NX))

    def sum_z(sign, step, name):
        first = 1 if (sign == "+") == (name[0] == "A") else 2
        offset = 5 - step if sign == "+" else step - 5
        cut = quarter_of(name)
        value = z_acc[offset % NZ, cut, :]
        mine = slot_of(sign, step, name)
        if step > first:
            arrive(f"z{sign}{step - 1}{name}")
            value = value + zr[slot_of(sign, step - 1, name)].astype(F32)
        zs[mine] = value.astype(BF16)
        send(f"z{sign}{step}{name}", zs.at[mine], zr.at[mine], at(dz=1 if sign == "+" else -1))

    quarter = rows // 4

    def quarter_of(name):
        return pl.ds((2 * (name[0] == "B") + int(name[1])) * quarter, quarter)

    def slot_of(sign, step, name):
        return (16 * (sign == "-") + 8 * (name[0] == "B") + 4 * int(name[1])) + step - 1

    def backward():
        arrive("r1", "r2", "r3")
        value = x_own[...]
        for j in (1, 3, 2):
            value = value + xr[j].astype(F32)
        grad_t[...] = value.astype(BF16)
        for h in range(heads):
            span = pl.ds(h * HD, HD)
            probs = probs_t[h]
            out_grad = grad_t[span, :]
            diagonal = jnp.sum(out_grad.astype(F32) * att_t[0, span, :].astype(F32), axis=0, keepdims=True)
            grad_probs = dot(v_v[:, span], out_grad, NN)
            grad_scores = (probs * (grad_probs - diagonal)).astype(BF16)
            gk_v[:, span] = (dot(grad_scores, q_v[:, span], NN) * scale).astype(BF16)
            gq_v[:, span] = (dot(grad_scores, k_v[:, span], TN) * scale).astype(BF16)
            gv_v[:, span] = dot(probs.astype(BF16), out_grad, NT).astype(BF16)

    def end_z():
        arrive(*(f"cz{d}" for d in range(1, NZ)))
        patches = cnt_z[0]
        for d in range(1, NZ):
            patches = patches + cnt_z[d]
        inverse = 1.0 / patches[0:1, 0:1]
        locals_["fisher"].wait()
        for name in ("B0", "B1", "A0", "A1"):
            cut = quarter_of(name)
            value = z_acc[0, cut, :]
            for sign in "+-":
                arrive(f"z{sign}4{name}")
                value = value + zr[slot_of(sign, 4, name)].astype(F32)
            wg_v[cut, :] = value
            fn_v[cut, :] = fisher_v[cut, :] + value * value * inverse

    for task in ORDER:
        if task == "start":
            start()
        elif task[:3] == "fwd":
            forward(int(task[3]))
        elif task == "at":
            share_attended()
        elif task[:6] == "spread":
            spread(int(task[6]), int(task[7]))
        elif task[:2] == "ry":
            relay_y(int(task[2]), task[3], int(task[4]))
        elif task[:2] == "ey":
            end_y(int(task[2]), int(task[3]))
        elif task[:2] == "rw":
            relay_w(task[2], int(task[3]), task[4])
        elif task == "counts":
            counts()
        elif task == "wt":
            end_w()
        elif task[:2] == "px":
            grad_part(int(task[2]))
        elif task[:2] == "pz":
            weight_part(int(task[2:]))
        elif task[:2] == "sz":
            sum_z(task[2], int(task[3]), task[4:])
        elif task == "bwd":
            backward()
        else:
            end_z()

    for copy in pending.values():
        copy.wait_send()


def copy_kernel(*refs):
    n = len(refs) // 2
    sem = refs[-1]
    copies = [pltpu.make_async_copy(refs[i], refs[n + i], sem.at[i]) for i in range(n)]
    for copy in copies:
        copy.start()
    for copy in copies:
        copy.wait()


def per_device(queries, keys, values, upstream, out_weight, fisher, image_lengths):
    tokens, width = queries.shape
    rows = out_weight.shape[0]
    heads = width // HD
    hbm = pl.BlockSpec(memory_space=pl.ANY)
    vm = pltpu.VMEM
    scratch = [
        vm((tokens, width), BF16),
        vm((tokens, width), BF16),
        vm((tokens, width), BF16),
        vm(upstream.shape, BF16),
        vm((rows, width), F32),
        vm((upstream.shape[1], tokens), BF16),
        vm((NX, NZ * rows, tokens), BF16),
        vm((NZ * rows, width), BF16),
        vm((width, NZ * rows), BF16),
        vm((NX, width, tokens), BF16),
        vm((heads, tokens, tokens), F32),
        vm((NX, width, tokens), BF16),
        vm((NX, width, tokens), BF16),
        vm((width, tokens), F32),
        vm((width, tokens), BF16),
        vm((32, rows // 4, width), BF16),
        vm((32, rows // 4, width), BF16),
        vm((NZ, rows, width), F32),
        vm((8, HD), F32),
        vm((NX, 8, HD), F32),
        vm((NZ, 8, HD), F32),
        pltpu.SMEM(image_lengths.shape, jnp.int32),
        pltpu.SemaphoreType.DMA((N_REMOTE,)),
        pltpu.SemaphoreType.DMA((N_REMOTE,)),
        pltpu.SemaphoreType.DMA((N_LOCAL,)),
    ]
    shapes = [((tokens, width), BF16)] * 3 + [((rows, width), F32)] * 2
    inputs = (image_lengths, queries, keys, values, upstream, out_weight, fisher)
    results = pl.pallas_call(
        kernel,
        out_shape=[pltpu.VMEM(*shape) for shape in shapes],
        in_specs=[hbm] * 7,
        out_specs=[pl.BlockSpec(memory_space=pltpu.VMEM)] * 5,
        scratch_shapes=scratch,
        compiler_params=pltpu.CompilerParams(
            collective_id=0, has_side_effects=True, vmem_limit_bytes=VMEM_LIMIT
        ),
    )(*(pltpu.with_memory_space_constraint(a, pltpu.HBM) for a in inputs))
    return pl.pallas_call(
        copy_kernel,
        out_shape=[pltpu.HBM(*shape) for shape in shapes],
        in_specs=[pl.BlockSpec(memory_space=pltpu.VMEM)] * 5,
        out_specs=[hbm] * 5,
        scratch_shapes=[pltpu.SemaphoreType.DMA((5,))],
        compiler_params=pltpu.CompilerParams(vmem_limit_bytes=VMEM_LIMIT),
    )(*(pltpu.with_memory_space_constraint(a, pltpu.VMEM) for a in results))


def solution(mesh):
    placed = P("dp", "tensor")
    return jax.shard_map(
        per_device,
        mesh=mesh,
        in_specs=(placed,) * 6 + (P("dp", None),),
        out_specs=(placed,) * 5,
        check_vma=False,
    )
```

time: 381 us -> 49.7 us (0.13)
  waiting for transfers between devices: 264 us -> 0 us
  blocking collectives: 67 us -> 0 us
  Pallas kernels: 0 us -> 49 us
  matrix products: 19.7 us -> 0 us
  between operations: 14.5 us -> 0.64 us
  local copies, waits for them, and re-layouts: 9.49 us -> 0 us
  other arithmetic: 4.92 us -> 0 us
    reduce_scatter x1 -> x0, waiting for transfers between devices: 151 us -> none  [per_device(): lax.psum_scatter(lax.dot_general(grad_masked, attended_all, contract_rows...]
    all_gather x2 -> x0, waiting for transfers between devices: 112 us -> none  [the longest x1 86.2 us: per_device(): lax.all_gather(out_weight, 'dp', axis=0, tiled=True)]
    psum x1 -> x0, blocking collectives: 67 us -> none  [per_device(): patch_total = lax.psum(filled.astype(jnp.float32), 'dp')]
    pallas_call x0 -> x2, Pallas kernels: none -> 49 us  [the longest x1 47.9 us: per_device(): pl.pallas_call(kernel, out_shape=[pltpu.VMEM(*shape) for shape in shapes]...]
    dot_general x14 -> x0, matrix products: 19.7 us -> none  [the longest x1 7.48 us: per_device(): lax.dot_general(grad_masked, attended_all, contract_rows, preferred_eleme...]
    unnamed x10 -> x0, local copies, waits for them, and re-layouts: 6.62 us -> none
  transfers between devices with their start and end apart: 3 -> 0, of which waited for: 3 -> 0; matrix products, arithmetic and copies ran while one was open for 5% -> 0% of each run, Pallas kernels for 0% -> 0%
where the time goes in v2:
time: 49.7 us; the launch traced here: 49.6 us
  Pallas kernels  49 us (99%)
  between operations  0.64 us (1%)
    pallas_call x1, Pallas kernels, per_device(): pl.pallas_call(kernel, out_shape=[pltpu.VMEM(*shape) for shape in shapes]...  47.9 us
    pallas_call x1, Pallas kernels, per_device(): pl.pallas_call(copy_kernel, out_shape=[pltpu.HBM(*shape) for shape in sha...  1.05 us

profile of v2, /device:TPU:32, one launch (start us, length us, event | category | flops | bytes accessed | tf_op | source)
XLA Modules:
  0.0 49.6 jit_solution(14731133294503141186)
XLA Ops:
  0.6 47.9 %shard_map.110 = (bf16[256,384]{1,0:T(8,128)(2,1)S(1)}, bf16[256,384]{1,0:T(8,128)(2,1)S(1)}, bf16[256,384]{1,0:T(8,128)(2,1)S(1)}, f32[192,384]{1,0:T(8,128)S(1)}, f32[192,384]{1,0:T(8,128)S(1)}) custom-call(s32[1,8]{1,0:T(1,128)} %len_hbm.1, bf16[256,384]{1,0:T(8,128)(2,1)} %q_hbm.1, bf16[256,384]{1,0:T(8,128)(2,1)} %k_hbm.1, bf16[256,384]{1,0:T(8,128)(2,1)} %v_hbm.1, ...), custom_call_target="tpu_custom_call" | custom-call | tf_op jit(solution)/shard_map/pallas_call | solution.py:356
  48.5 1.1 %shard_map.111 = (bf16[256,384]{1,0:T(8,128)(2,1)}, bf16[256,384]{1,0:T(8,128)(2,1)}, bf16[256,384]{1,0:T(8,128)(2,1)}, f32[192,384]{1,0:T(8,128)}, f32[192,384]{1,0:T(8,128)}) custom-call(bf16[256,384]{1,0:T(8,128)(2,1)S(1)} %get-tuple-element.10.refs_0_, bf16[256,384]{1,0:T(8,128)(2,1)S(1)} %get-tuple-element.11.refs_1_, ...), custom_call_target="tpu_custom_call" | custom-call | tf_op jit(solution)/shard_map/pallas_call | solution.py:366

commit v3 on v2

--- a/solution.py
+++ b/solution.py
@@ -12,19 +12,22 @@
 NX, NY, NZ = 4, 4, 8
 FLOOR_SCORE = -1e30
 F32, BF16 = jnp.float32, jnp.bfloat16
-N_REMOTE = 128
-N_LOCAL = 16
+H = 2
+Q = 2
+N_REMOTE = 28 + 15 * H + 14 * Q
+N_LOCAL = 7
 VMEM_LIMIT = 48 * 1024 * 1024
 
 ORDER = (
     "start", "fwd0", "fwd1", "fwd2", "at", "spread30", "ry0+0", "ry0-0", "spread10", "rw+2A", "rw-2B",
     "spread31", "ry0+1", "ry0-1", "spread11", "rw+2B", "rw-2A", "spread20", "ry3+0", "ry3-0", "spread21",
     "rw+3A", "rw-3B", "ey00", "ry1-0", "ry1+0", "ry3-1", "rw+3B", "rw-3A", "ry3+1", "ey01", "ry1+1", "ry1-1",
-    "rw+4A", "rw-4B", "counts", "ry2+0", "ry2-0", "ey30", "ry2-1", "ry2+1", "ey31", "wt", "ey10", "ey11",
-    "px3", "ey20", "ey21", "px1", "px2", "px0", "pz4", "sz+1A0", "sz+1A1", "sz-1B0", "sz-1B1", "pz3",
-    "sz+2B0", "sz+2B1", "pz-3", "sz-2A0", "sz-2A1", "pz2", "pz-2", "pz1", "pz-1", "pz0", "sz+2A0", "sz-2B0",
-    "sz+2A1", "sz-2B1", "sz+3B0", "sz-3A0", "sz+3B1", "sz-3A1", "sz+3A0", "sz-3B0", "sz+3A1", "sz-3B1",
-    "sz+4B0", "sz-4A0", "sz+4B1", "sz-4A1", "sz+4A0", "sz-4B0", "sz+4A1", "sz-4B1", "bwd", "end",
+    "rw+4A", "rw-4B", "ry2+0", "ry2-0", "ey30", "ry2-1", "ry2+1", "ey31", "c4", "ey10", "ey11", "ey20",
+    "ey21", "wt", "ec3", "px3", "ec1", "px1", "enda", "ec0", "ec2", "pz4", "sz+1A0", "sz+1A1", "sz-1B0",
+    "sz-1B1", "pz3", "sz+2B0", "sz+2B1", "pz-3", "sz-2A0", "sz-2A1", "px2", "pz2", "pz-2", "sz+2A0", "sz-2B0",
+    "sz+2A1", "sz-2B1", "pz1", "pz-1", "cx", "px0", "sz+3B0", "sz-3A0", "sz+3B1", "sz-3A1", "sz+3A0",
+    "sz-3B0", "sz+3A1", "sz-3B1", "pz0", "sz+4B0", "sz-4A0", "sz+4B1", "sz-4A1", "sz+4A0", "sz-4B0", "sz+4A1",
+    "sz-4B1", "bwd", "end",
 )
 
 NN = (((1,), (0,)), ((), ()))
@@ -40,7 +43,7 @@
     len_hbm, q_hbm, k_hbm, v_hbm, up_hbm, w_hbm, fisher_hbm,
     gq_v, gk_v, gv_v, wg_v, fn_v,
     q_v, k_v, v_v, up_v, fisher_v,
-    up_t, g_all, w_all, w_t, att_t, probs_t,
+    up_t, g_all, w_all, att_t, probs_t,
     xs, xr, x_own, grad_t,
     zs, zr, z_acc, cnt, cnt_x, cnt_z, len_ref,
     send_sem, recv_sem, local_sem,
@@ -64,11 +67,16 @@
         return pl.ds(pl.multiple_of(index * rows + start, 16), size)
 
     pending = {}
+    receivers = {}
+    senders = {"w": [], "c": [], "g": [], "a": [], "r": [], "x": [], "z": []}
 
     def send(name, src, dst, to):
-        number = len(pending)
+        kind = "g" if name[0] in "gys" else "x" if name[:2] == "cx" else name[0]
+        shared = name[:2] if name[0] == "s" else kind if kind in "arx" else name
+        senders[kind].append(name)
         copy = pltpu.make_async_remote_copy(
-            src_ref=src, dst_ref=dst, send_sem=send_sem.at[number], recv_sem=recv_sem.at[number],
+            src_ref=src, dst_ref=dst, send_sem=send_sem.at[list(senders).index(kind)],
+            recv_sem=recv_sem.at[receivers.setdefault(shared, len(receivers))],
             device_id=to, device_id_type=MESH,
         )
         copy.start()
@@ -78,12 +86,23 @@
         for name in names:
             pending[name].wait_recv()
 
+    def all_of(kind, ref, shared):
+        return pltpu.make_async_remote_copy(
+            src_ref=ref, dst_ref=ref, send_sem=send_sem.at[list(senders).index(kind)],
+            recv_sem=recv_sem.at[receivers[shared]], device_id=at(other=True), device_id_type=MESH,
+        )
+
     locals_ = {}
 
     def load(name, src, dst):
         copy = pltpu.make_async_copy(src, dst, local_sem.at[len(locals_)])
         copy.start()
         locals_[name] = copy
+
+    peers = [at(dz=1), at(dz=-1), at(dx=1), at(dx=2), at(dx=3), at(dy=1), at(dy=-1), at(other=True)]
+    barrier = pltpu.get_barrier_semaphore()
+    for peer in peers:
+        pl.semaphore_signal(barrier, inc=1, device_id=peer, device_id_type=MESH)
 
     load("len", len_hbm, len_ref)
     load("up", up_hbm, up_v)
@@ -93,11 +112,14 @@
     load("w", w_hbm, w_all.at[block(z)])
     load("fisher", fisher_hbm, fisher_v)
 
-    peers = [at(dz=d) for d in range(1, NZ)] + [at(dx=d) for d in range(1, NX)]
-    peers += [at(dy=1), at(dy=-1), at(other=True)]
-    barrier = pltpu.get_barrier_semaphore()
-    for peer in peers:
-        pl.semaphore_signal(barrier, inc=1, device_id=peer, device_id_type=MESH)
+    def w_rows(index, part):
+        return w_all.at[block(index, 0 if part == "A" else half, half)]
+
+    pl.semaphore_wait(barrier, len(peers))
+    for part, cut in (("A", pl.ds(0, half)), ("B", pl.ds(half, half))):
+        send(f"w+1{part}", w_hbm.at[cut], w_rows(z, part), at(dz=1))
+    for part, cut in (("B", pl.ds(half, half)), ("A", pl.ds(0, half))):
+        send(f"w-1{part}", w_hbm.at[cut], w_rows(z, part), at(dz=-1))
 
     locals_["len"].wait()
     finish = []
@@ -106,7 +128,6 @@
         total = total + len_ref[0, j]
         finish.append(total)
     filled = finish[-1]
-    cnt[...] = jnp.full(cnt.shape, filled.astype(F32), F32)
 
     u_position = lax.broadcasted_iota(jnp.int32, (tokens, 1), 0)
     t_position = lax.broadcasted_iota(jnp.int32, (1, tokens), 1)
@@ -122,19 +143,25 @@
         piece = up_v[:, j * HD:(j + 1) * HD].astype(F32)
         up_t[j * HD:(j + 1) * HD, :] = jnp.where(inside, piece, 0.0).T.astype(BF16)
     g_all[0, block(tau), :] = up_t[block(x), :]
-    pl.semaphore_wait(barrier, len(peers))
-
-    def w_rows(index, part):
-        return w_all.at[block(index, 0 if part == "A" else half, half)]
+
+    def hand_count(sign, step):
+        one = 1 if sign == "+" else -1
+        if step > 1:
+            arrive(f"c{sign}{step - 1}")
+        send(f"c{sign}{step}", cnt_z.at[one * (step - 1) % NZ], cnt_z.at[one * step % NZ], at(dz=one))
 
     def relay_w(sign, step, part):
         arrive(f"w{sign}{step - 1}{part}")
         one = 1 if sign == "+" else -1
         rows_there = w_rows((z - one * (step - 1) + NZ) % NZ, part)
         send(f"w{sign}{step}{part}", rows_there, rows_there, at(dz=one))
+        if part == ("B" if sign == "+" else "A"):
+            hand_count(sign, step)
+
+    piece_rows = rows // H
 
     def g_rows(slot, dy, part):
-        return g_all.at[slot, block(((y + dy + NY) % NY) * 2 + c, part * half, half)]
+        return g_all.at[slot, block(((y + dy + NY) % NY) * 2 + c, part * piece_rows, piece_rows)]
 
     def spread(slot, part):
         if slot:
@@ -148,35 +175,30 @@
         arrive(f"y{slot}{sign}{part}")
         one = 1 if sign == "+" else -1
         piece = g_rows(slot, -one, part)
-        if (part == 0) == (sign == "+"):
+        if (part < H // 2) == (sign == "+"):
             send(f"y{slot}{sign}{part}F", piece, piece, at(dy=one))
         send(f"s{slot}{sign}{part}", piece, piece, at(other=True))
 
     def end_y(slot, part):
-        arrive(f"y{slot}{'+' if part == 0 else '-'}{part}F")
+        arrive(f"y{slot}{'+' if part < H // 2 else '-'}{part}F")
         piece = g_rows(slot, 2, part)
         send(f"s{slot}3{part}", piece, piece, at(other=True))
 
     def end_core(slot):
-        for j in "0+-3":
-            for part in (0, 1):
-                arrive(f"s{slot}{j}{part}")
+        all_of("g", g_all.at[slot, pl.ds(0, 4 * rows)], f"s{slot}").wait_recv()
 
     def start():
-        for part, cut in (("A", pl.ds(0, half)), ("B", pl.ds(half, half))):
-            send(f"w+1{part}", w_hbm.at[cut], w_rows(z, part), at(dz=1))
-        for part, cut in (("B", pl.ds(half, half)), ("A", pl.ds(0, half))):
-            send(f"w-1{part}", w_hbm.at[cut], w_rows(z, part), at(dz=-1))
-        for part in (0, 1):
+        for part in range(H):
             for slot, dx in ((3, 1), (1, -1)):
-                there = (x + dx + NX) % NX
-                send(f"g{slot}{part}", up_t.at[block(there, part * half, half)], g_rows(slot, 0, part), at(dx=dx))
+                there = block((x + dx + NX) % NX, part * piece_rows, piece_rows)
+                send(f"g{slot}{part}", up_t.at[there], g_rows(slot, 0, part), at(dx=dx))
             spread(0, part)
-        for part in (0, 1):
-            there = (x + 2) % NX
-            send(f"g2{part}", up_t.at[block(there, part * half, half)], g_rows(2, 0, part), at(dx=2))
-        for d in range(1, NX):
-            send(f"cx{d}", cnt, cnt_x.at[d], at(dx=d))
+        for part in range(H):
+            there = block((x + 2) % NX, part * piece_rows, piece_rows)
+            send(f"g2{part}", up_t.at[there], g_rows(2, 0, part), at(dx=2))
+        cnt_z[0] = jnp.full(cnt.shape, filled.astype(F32), F32)
+        hand_count("+", 1)
+        hand_count("-", 1)
         for name in ("q", "k", "v"):
             locals_[name].wait()
 
@@ -194,21 +216,18 @@
         for d in (1, 3, 2):
             send(f"a{d}", att_t.at[0], att_t.at[(NX - d) % NX], at(dx=d))
 
-    def counts():
-        arrive(*(f"cx{d}" for d in range(1, NX)))
-        cnt_z[0] = cnt[...] + cnt_x[1] + cnt_x[2] + cnt_x[3]
-        for d in range(1, NZ):
-            send(f"cz{d}", cnt_z.at[0], cnt_z.at[d], at(dz=d))
-
     def end_w():
         arrive("w+3B", "w-3A", "w+4A", "w-4B")
         locals_["w"].wait()
-        for j in range(w_all.shape[0] // HD):
-            w_t[:, j * HD:(j + 1) * HD] = w_all[j * HD:(j + 1) * HD, :].T
+
+    def counts():
+        arrive("c+4", "c-3")
+        cnt[...] = sum(cnt_z[d] for d in range(NZ))
+        for d in range(1, NX):
+            send(f"cx{d}", cnt, cnt_x.at[d], at(dx=d))
 
     def grad_part(slot):
-        end_core(slot)
-        term = dot(w_t[...], g_all[slot], NN)
+        term = dot(w_all[...], g_all[slot], TN)
         if slot == 0:
             x_own[...] = term
         else:
@@ -216,8 +235,6 @@
             send(f"r{slot}", xs.at[slot], xr.at[slot], at(dx=slot))
 
     def weight_part(offset):
-        if offset == 4:
-            arrive("a1", "a2", "a3")
         target = (z + offset + NZ) % NZ
         z_acc[offset % NZ] = sum(dot(g_all[j, block(target), :], att_t[j], NT) for j in range(NX))
 
@@ -233,16 +250,16 @@
         zs[mine] = value.astype(BF16)
         send(f"z{sign}{step}{name}", zs.at[mine], zr.at[mine], at(dz=1 if sign == "+" else -1))
 
-    quarter = rows // 4
+    quarter = rows // (2 * Q)
 
     def quarter_of(name):
-        return pl.ds((2 * (name[0] == "B") + int(name[1])) * quarter, quarter)
+        return pl.ds((Q * (name[0] == "B") + int(name[1])) * quarter, quarter)
 
     def slot_of(sign, step, name):
-        return (16 * (sign == "-") + 8 * (name[0] == "B") + 4 * int(name[1])) + step - 1
+        return ((2 * (sign == "-") + (name[0] == "B")) * Q + int(name[1])) * 4 + step - 1
 
     def backward():
-        arrive("r1", "r2", "r3")
+        all_of("r", xr.at[pl.ds(1, NX - 1)], "r").wait_recv()
         value = x_own[...]
         for j in (1, 3, 2):
             value = value + xr[j].astype(F32)
@@ -259,13 +276,13 @@
             gv_v[:, span] = dot(probs.astype(BF16), out_grad, NT).astype(BF16)
 
     def end_z():
-        arrive(*(f"cz{d}" for d in range(1, NZ)))
-        patches = cnt_z[0]
-        for d in range(1, NZ):
-            patches = patches + cnt_z[d]
+        all_of("x", cnt_x.at[pl.ds(1, NX - 1)], "x").wait_recv()
+        patches = cnt[...]
+        for d in range(1, NX):
+            patches = patches + cnt_x[d]
         inverse = 1.0 / patches[0:1, 0:1]
         locals_["fisher"].wait()
-        for name in ("B0", "B1", "A0", "A1"):
+        for name in [part + str(j) for part in "BA" for j in range(Q)]:
             cut = quarter_of(name)
             value = z_acc[0, cut, :]
             for sign in "+-":
@@ -289,7 +306,13 @@
             end_y(int(task[2]), int(task[3]))
         elif task[:2] == "rw":
             relay_w(task[2], int(task[3]), task[4])
-        elif task == "counts":
+        elif task == "enda":
+            all_of("a", att_t.at[pl.ds(1, NX - 1)], "a").wait_recv()
+        elif task[:2] == "ec":
+            end_core(int(task[2]))
+        elif task == "c4":
+            hand_count("+", 4)
+        elif task == "cx":
             counts()
         elif task == "wt":
             end_w()
@@ -304,8 +327,17 @@
         else:
             end_z()
 
-    for copy in pending.values():
-        copy.wait_send()
+    pieces = len(senders["g"]) * piece_rows // NX
+    for kind, ref in (
+        ("w", w_all.at[pl.ds(0, len(senders["w"]) * half)]),
+        ("c", cnt_z.at[pl.ds(0, len(senders["c"]))]),
+        ("g", g_all.at[:, pl.ds(0, pieces)]),
+        ("a", att_t.at[pl.ds(0, NX - 1)]),
+        ("r", xs.at[pl.ds(0, NX - 1)]),
+        ("x", cnt_x.at[pl.ds(0, NX - 1)]),
+        ("z", zs.at[pl.ds(0, len(senders["z"]))]),
+    ):
+        all_of(kind, ref, "a").wait_send()
 
 
 def copy_kernel(*refs):
@@ -333,21 +365,20 @@
         vm((upstream.shape[1], tokens), BF16),
         vm((NX, NZ * rows, tokens), BF16),
         vm((NZ * rows, width), BF16),
-        vm((width, NZ * rows), BF16),
         vm((NX, width, tokens), BF16),
         vm((heads, tokens, tokens), F32),
         vm((NX, width, tokens), BF16),
         vm((NX, width, tokens), BF16),
         vm((width, tokens), F32),
         vm((width, tokens), BF16),
-        vm((32, rows // 4, width), BF16),
-        vm((32, rows // 4, width), BF16),
+        vm((16 * Q, rows // (2 * Q), width), BF16),
+        vm((16 * Q, rows // (2 * Q), width), BF16),
         vm((NZ, rows, width), F32),
         vm((8, HD), F32),
         vm((NX, 8, HD), F32),
         vm((NZ, 8, HD), F32),
         pltpu.SMEM(image_lengths.shape, jnp.int32),
-        pltpu.SemaphoreType.DMA((N_REMOTE,)),
+        pltpu.SemaphoreType.DMA((7,)),
         pltpu.SemaphoreType.DMA((N_REMOTE,)),
         pltpu.SemaphoreType.DMA((N_LOCAL,)),
     ]

time: 49.7 us -> 45.3 us (0.911)
  Pallas kernels: 49 us -> 44.4 us
    pallas_call x1, Pallas kernels: 47.9 us -> 43.3 us  [per_device(): pl.pallas_call(kernel, out_shape=[pltpu.VMEM(*shape) for shape in shapes]...]
where the time goes in v3:
time: 45.3 us; the launch traced here: 45 us
  Pallas kernels  44.4 us (98%)
  between operations  0.64 us (1%)
    pallas_call x1, Pallas kernels, per_device(): pl.pallas_call(kernel, out_shape=[pltpu.VMEM(*shape) for shape in shapes]...  43.3 us
    pallas_call x1, Pallas kernels, per_device(): pl.pallas_call(copy_kernel, out_shape=[pltpu.HBM(*shape) for shape in sha...  1.05 us

profile of v3, /device:TPU:32, one launch (start us, length us, event | category | flops | bytes accessed | tf_op | source)
XLA Modules:
  0.0 45.0 jit_solution(18264924126287649560)
XLA Ops:
  0.6 43.3 %shard_map.110 = (bf16[256,384]{1,0:T(8,128)(2,1)S(1)}, bf16[256,384]{1,0:T(8,128)(2,1)S(1)}, bf16[256,384]{1,0:T(8,128)(2,1)S(1)}, f32[192,384]{1,0:T(8,128)S(1)}, f32[192,384]{1,0:T(8,128)S(1)}) custom-call(s32[1,8]{1,0:T(1,128)} %len_hbm.1, bf16[256,384]{1,0:T(8,128)(2,1)} %q_hbm.1, bf16[256,384]{1,0:T(8,128)(2,1)} %k_hbm.1, bf16[256,384]{1,0:T(8,128)(2,1)} %v_hbm.1, ...), custom_call_target="tpu_custom_call" | custom-call | tf_op jit(solution)/shard_map/pallas_call | solution.py:387
  44.0 1.1 %shard_map.111 = (bf16[256,384]{1,0:T(8,128)(2,1)}, bf16[256,384]{1,0:T(8,128)(2,1)}, bf16[256,384]{1,0:T(8,128)(2,1)}, f32[192,384]{1,0:T(8,128)}, f32[192,384]{1,0:T(8,128)}) custom-call(bf16[256,384]{1,0:T(8,128)(2,1)S(1)} %get-tuple-element.10.refs_0_, bf16[256,384]{1,0:T(8,128)(2,1)S(1)} %get-tuple-element.11.refs_1_, ...), custom_call_target="tpu_custom_call" | custom-call | tf_op jit(solution)/shard_map/pallas_call | solution.py:397

commit v4 on v3

--- a/solution.py
+++ b/solution.py
@@ -13,21 +13,22 @@
 FLOOR_SCORE = -1e30
 F32, BF16 = jnp.float32, jnp.bfloat16
 H = 2
-Q = 2
+Q = 3
 N_REMOTE = 28 + 15 * H + 14 * Q
 N_LOCAL = 7
 VMEM_LIMIT = 48 * 1024 * 1024
 
 ORDER = (
-    "start", "fwd0", "fwd1", "fwd2", "at", "spread30", "ry0+0", "ry0-0", "spread10", "rw+2A", "rw-2B",
-    "spread31", "ry0+1", "ry0-1", "spread11", "rw+2B", "rw-2A", "spread20", "ry3+0", "ry3-0", "spread21",
-    "rw+3A", "rw-3B", "ey00", "ry1-0", "ry1+0", "ry3-1", "rw+3B", "rw-3A", "ry3+1", "ey01", "ry1+1", "ry1-1",
-    "rw+4A", "rw-4B", "ry2+0", "ry2-0", "ey30", "ry2-1", "ry2+1", "ey31", "c4", "ey10", "ey11", "ey20",
-    "ey21", "wt", "ec3", "px3", "ec1", "px1", "enda", "ec0", "ec2", "pz4", "sz+1A0", "sz+1A1", "sz-1B0",
-    "sz-1B1", "pz3", "sz+2B0", "sz+2B1", "pz-3", "sz-2A0", "sz-2A1", "px2", "pz2", "pz-2", "sz+2A0", "sz-2B0",
-    "sz+2A1", "sz-2B1", "pz1", "pz-1", "cx", "px0", "sz+3B0", "sz-3A0", "sz+3B1", "sz-3A1", "sz+3A0",
-    "sz-3B0", "sz+3A1", "sz-3B1", "pz0", "sz+4B0", "sz-4A0", "sz+4B1", "sz-4A1", "sz+4A0", "sz-4B0", "sz+4A1",
-    "sz-4B1", "bwd", "end",
+    "fwd0", "fwd1", "fwd2", "at", "spread30", "ry0+0", "ry0-0", "spread10", "rw+2A", "rw-2B", "spread31",
+    "ry0+1", "ry0-1", "spread11", "rw+2B", "rw-2A", "spread20", "ry3+0", "ry3-0", "spread21", "rw+3A",
+    "rw-3B", "ey00", "ry1-0", "ry1+0", "ry3-1", "rw+3B", "rw-3A", "ry3+1", "ey01", "ry1+1", "ry1-1", "rw+4A",
+    "rw-4B", "ry2+0", "ry2-0", "ey30", "ry2-1", "ry2+1", "ey31", "c4", "ey10", "ey11", "ey20", "ey21", "enda",
+    "ec0", "ec3", "ec1", "pzp", "wt", "px3", "px1", "ec2", "pzq", "sz+1A0", "sz+1A1", "sz+1A2", "sz-1B0",
+    "sz-1B1", "sz-1B2", "pz3", "sz+2B0", "sz+2B1", "sz+2B2", "pz-3", "sz-2A0", "sz-2A1", "sz-2A2", "px2",
+    "pz2", "pz-2", "sz+2A0", "sz-2B0", "sz+2A1", "sz-2B1", "sz+2A2", "sz-2B2", "pz1", "pz-1", "cx", "sz+3B0",
+    "sz-3A0", "sz+3B1", "sz-3A1", "sz+3B2", "sz-3A2", "sz+3A0", "sz-3B0", "sz+3A1", "sz-3B1", "sz+3A2",
+    "sz-3B2", "sz+4B0", "sz-4A0", "sz+4B1", "sz-4A1", "sz+4B2", "sz-4A2", "sz+4A0", "sz-4B0", "sz+4A1",
+    "sz-4B1", "sz+4A2", "sz-4B2", "px0", "pz0", "bwd", "end",
 )
 
 NN = (((1,), (0,)), ((), ()))
@@ -104,45 +105,17 @@
     for peer in peers:
         pl.semaphore_signal(barrier, inc=1, device_id=peer, device_id_type=MESH)
 
+    load("up", up_hbm, up_v)
     load("len", len_hbm, len_ref)
-    load("up", up_hbm, up_v)
-    load("q", q_hbm, q_v)
-    load("k", k_hbm, k_v)
-    load("v", v_hbm, v_v)
-    load("w", w_hbm, w_all.at[block(z)])
-    load("fisher", fisher_hbm, fisher_v)
 
     def w_rows(index, part):
         return w_all.at[block(index, 0 if part == "A" else half, half)]
 
+    locals_["up"].wait()
+    for j in range(up_v.shape[1] // HD):
+        up_t[j * HD:(j + 1) * HD, :] = up_v[:, j * HD:(j + 1) * HD].T
+    g_all[0, block(tau), :] = up_t[block(x), :]
     pl.semaphore_wait(barrier, len(peers))
-    for part, cut in (("A", pl.ds(0, half)), ("B", pl.ds(half, half))):
-        send(f"w+1{part}", w_hbm.at[cut], w_rows(z, part), at(dz=1))
-    for part, cut in (("B", pl.ds(half, half)), ("A", pl.ds(0, half))):
-        send(f"w-1{part}", w_hbm.at[cut], w_rows(z, part), at(dz=-1))
-
-    locals_["len"].wait()
-    finish = []
-    total = jnp.int32(0)
-    for j in range(len_ref.shape[1]):
-        total = total + len_ref[0, j]
-        finish.append(total)
-    filled = finish[-1]
-
-    u_position = lax.broadcasted_iota(jnp.int32, (tokens, 1), 0)
-    t_position = lax.broadcasted_iota(jnp.int32, (1, tokens), 1)
-    u_segment = jnp.zeros((tokens, 1), jnp.int32)
-    t_segment = jnp.zeros((1, tokens), jnp.int32)
-    for end in finish:
-        u_segment += (u_position >= end).astype(jnp.int32)
-        t_segment += (t_position >= end).astype(jnp.int32)
-
-    locals_["up"].wait()
-    inside = lax.broadcasted_iota(jnp.int32, (tokens, HD), 0) < filled
-    for j in range(up_v.shape[1] // HD):
-        piece = up_v[:, j * HD:(j + 1) * HD].astype(F32)
-        up_t[j * HD:(j + 1) * HD, :] = jnp.where(inside, piece, 0.0).T.astype(BF16)
-    g_all[0, block(tau), :] = up_t[block(x), :]
 
     def hand_count(sign, step):
         one = 1 if sign == "+" else -1
@@ -196,11 +169,15 @@
         for part in range(H):
             there = block((x + 2) % NX, part * piece_rows, piece_rows)
             send(f"g2{part}", up_t.at[there], g_rows(2, 0, part), at(dx=2))
-        cnt_z[0] = jnp.full(cnt.shape, filled.astype(F32), F32)
-        hand_count("+", 1)
-        hand_count("-", 1)
-        for name in ("q", "k", "v"):
-            locals_[name].wait()
+        for part, cut in (("A", pl.ds(0, half)), ("B", pl.ds(half, half))):
+            send(f"w+1{part}", w_hbm.at[cut], w_rows(z, part), at(dz=1))
+        for part, cut in (("B", pl.ds(half, half)), ("A", pl.ds(0, half))):
+            send(f"w-1{part}", w_hbm.at[cut], w_rows(z, part), at(dz=-1))
+        for name, src, dst in (
+            ("q", q_hbm, q_v), ("k", k_hbm, k_v), ("v", v_hbm, v_v),
+            ("w", w_hbm, w_all.at[block(z)]), ("fisher", fisher_hbm, fisher_v),
+        ):
+            load(name, src, dst)
 
     def forward(h):
         span = pl.ds(h * HD, HD)
@@ -210,7 +187,8 @@
         weights = jnp.exp(shifted - largest)
         probs = weights * (1.0 / jnp.sum(weights, axis=0, keepdims=True))
         probs_t[h] = probs
-        att_t[0, span, :] = dot(v_v[:, span], probs.astype(BF16), TN).astype(BF16)
+        attended = dot(v_v[:, span], probs.astype(BF16), TN)
+        att_t[0, span, :] = jnp.where(t_position < filled, attended, 0.0).astype(BF16)
 
     def share_attended():
         for d in (1, 3, 2):
@@ -234,9 +212,12 @@
             xs[slot] = term.astype(BF16)
             send(f"r{slot}", xs.at[slot], xr.at[slot], at(dx=slot))
 
-    def weight_part(offset):
+    def weight_part(offset, slots=range(NX), more=False):
         target = (z + offset + NZ) % NZ
-        z_acc[offset % NZ] = sum(dot(g_all[j, block(target), :], att_t[j], NT) for j in range(NX))
+        term = sum(dot(g_all[j, block(target), :], att_t[j], NT) for j in slots)
+        if more:
+            term = z_acc[offset % NZ] + term
+        z_acc[offset % NZ] = term
 
     def sum_z(sign, step, name):
         first = 1 if (sign == "+") == (name[0] == "A") else 2
@@ -263,7 +244,7 @@
         value = x_own[...]
         for j in (1, 3, 2):
             value = value + xr[j].astype(F32)
-        grad_t[...] = value.astype(BF16)
+        grad_t[...] = jnp.where(t_position < filled, value, 0.0).astype(BF16)
         for h in range(heads):
             span = pl.ds(h * HD, HD)
             probs = probs_t[h]
@@ -291,10 +272,28 @@
             wg_v[cut, :] = value
             fn_v[cut, :] = fisher_v[cut, :] + value * value * inverse
 
+    start()
+    locals_["len"].wait()
+    finish = []
+    total = jnp.int32(0)
+    for j in range(len_ref.shape[1]):
+        total = total + len_ref[0, j]
+        finish.append(total)
+    filled = finish[-1]
+    u_position = lax.broadcasted_iota(jnp.int32, (tokens, 1), 0)
+    t_position = lax.broadcasted_iota(jnp.int32, (1, tokens), 1)
+    u_segment = jnp.zeros((tokens, 1), jnp.int32)
+    t_segment = jnp.zeros((1, tokens), jnp.int32)
+    for end in finish:
+        u_segment += (u_position >= end).astype(jnp.int32)
+        t_segment += (t_position >= end).astype(jnp.int32)
+    cnt_z[0] = jnp.full(cnt.shape, filled.astype(F32), F32)
+    hand_count("+", 1)
+    hand_count("-", 1)
+    for name in ("q", "k", "v"):
+        locals_[name].wait()
     for task in ORDER:
-        if task == "start":
-            start()
-        elif task[:3] == "fwd":
+        if task[:3] == "fwd":
             forward(int(task[3]))
         elif task == "at":
             share_attended()
@@ -318,6 +317,10 @@
             end_w()
         elif task[:2] == "px":
             grad_part(int(task[2]))
+        elif task == "pzp":
+            weight_part(4, (0, 1, 3))
+        elif task == "pzq":
+            weight_part(4, (2,), True)
         elif task[:2] == "pz":
             weight_part(int(task[2:]))
         elif task[:2] == "sz":

time: 45.3 us -> 44.1 us (0.974); the launches traced: 45 us -> 43.3 us
  Pallas kernels: 44.4 us -> 42.7 us
    pallas_call x1, Pallas kernels: 43.3 us -> 41.6 us  [per_device(): pl.pallas_call(kernel, out_shape=[pltpu.VMEM(*shape) for shape in shapes]...]
where the time goes in v4:
time: 44.1 us; the launch traced here: 43.3 us
  Pallas kernels  42.7 us (97%)
  between operations  0.64 us (1%)
    pallas_call x1, Pallas kernels, per_device(): pl.pallas_call(kernel, out_shape=[pltpu.VMEM(*shape) for shape in shapes]...  41.6 us
    pallas_call x1, Pallas kernels, per_device(): pl.pallas_call(copy_kernel, out_shape=[pltpu.HBM(*shape) for shape in sha...  1.05 us

profile of v4, /device:TPU:32, one launch (start us, length us, event | category | flops | bytes accessed | tf_op | source)
XLA Modules:
  0.0 43.3 jit_solution(5001131754976477011)
XLA Ops:
  0.6 41.6 %shard_map.110 = (bf16[256,384]{1,0:T(8,128)(2,1)S(1)}, bf16[256,384]{1,0:T(8,128)(2,1)S(1)}, bf16[256,384]{1,0:T(8,128)(2,1)S(1)}, f32[192,384]{1,0:T(8,128)S(1)}, f32[192,384]{1,0:T(8,128)S(1)}) custom-call(s32[1,8]{1,0:T(1,128)} %len_hbm.1, bf16[256,384]{1,0:T(8,128)(2,1)} %q_hbm.1, bf16[256,384]{1,0:T(8,128)(2,1)} %k_hbm.1, bf16[256,384]{1,0:T(8,128)(2,1)} %v_hbm.1, ...), custom_call_target="tpu_custom_call" | custom-call | tf_op jit(solution)/shard_map/pallas_call | solution.py:390
  42.2 1.1 %shard_map.111 = (bf16[256,384]{1,0:T(8,128)(2,1)}, bf16[256,384]{1,0:T(8,128)(2,1)}, bf16[256,384]{1,0:T(8,128)(2,1)}, f32[192,384]{1,0:T(8,128)}, f32[192,384]{1,0:T(8,128)}) custom-call(bf16[256,384]{1,0:T(8,128)(2,1)S(1)} %get-tuple-element.10.refs_0_, bf16[256,384]{1,0:T(8,128)(2,1)S(1)} %get-tuple-element.11.refs_1_, ...), custom_call_target="tpu_custom_call" | custom-call | tf_op jit(solution)/shard_map/pallas_call | solution.py:400

commit v5 on v4

--- a/solution.py
+++ b/solution.py
@@ -13,9 +13,9 @@
 FLOOR_SCORE = -1e30
 F32, BF16 = jnp.float32, jnp.bfloat16
 H = 2
-Q = 3
+Q = 2
 N_REMOTE = 28 + 15 * H + 14 * Q
-N_LOCAL = 7
+N_LOCAL = 8
 VMEM_LIMIT = 48 * 1024 * 1024
 
 ORDER = (
@@ -23,12 +23,11 @@
     "ry0+1", "ry0-1", "spread11", "rw+2B", "rw-2A", "spread20", "ry3+0", "ry3-0", "spread21", "rw+3A",
     "rw-3B", "ey00", "ry1-0", "ry1+0", "ry3-1", "rw+3B", "rw-3A", "ry3+1", "ey01", "ry1+1", "ry1-1", "rw+4A",
     "rw-4B", "ry2+0", "ry2-0", "ey30", "ry2-1", "ry2+1", "ey31", "c4", "ey10", "ey11", "ey20", "ey21", "enda",
-    "ec0", "ec3", "ec1", "pzp", "wt", "px3", "px1", "ec2", "pzq", "sz+1A0", "sz+1A1", "sz+1A2", "sz-1B0",
-    "sz-1B1", "sz-1B2", "pz3", "sz+2B0", "sz+2B1", "sz+2B2", "pz-3", "sz-2A0", "sz-2A1", "sz-2A2", "px2",
-    "pz2", "pz-2", "sz+2A0", "sz-2B0", "sz+2A1", "sz-2B1", "sz+2A2", "sz-2B2", "pz1", "pz-1", "cx", "sz+3B0",
-    "sz-3A0", "sz+3B1", "sz-3A1", "sz+3B2", "sz-3A2", "sz+3A0", "sz-3B0", "sz+3A1", "sz-3B1", "sz+3A2",
-    "sz-3B2", "sz+4B0", "sz-4A0", "sz+4B1", "sz-4A1", "sz+4B2", "sz-4A2", "sz+4A0", "sz-4B0", "sz+4A1",
-    "sz-4B1", "sz+4A2", "sz-4B2", "px0", "pz0", "bwd", "end",
+    "ec0", "ec3", "ec1", "pzp", "wt", "px3", "px1", "ec2", "pzq", "sz+1A0", "sz-1B0", "sz+1A1", "sz-1B1",
+    "pz3", "pz-3", "sz+2B0", "sz-2A0", "sz+2B1", "sz-2A1", "px2", "pz2", "pz-2", "sz+2A0", "sz-2B0", "sz+2A1",
+    "sz-2B1", "pz1", "pz-1", "cx", "sz+3B0", "sz-3A0", "sz+3B1", "sz-3A1", "sz+3A0", "sz-3B0", "sz+3A1",
+    "sz-3B1", "sz+4B0", "sz-4A0", "sz+4B1", "sz-4A1", "sz+4A0", "sz-4B0", "sz+4A1", "sz-4B1", "px0", "pz0",
+    "bwd", "end",
 )
 
 NN = (((1,), (0,)), ((), ()))
@@ -105,15 +104,17 @@
     for peer in peers:
         pl.semaphore_signal(barrier, inc=1, device_id=peer, device_id_type=MESH)
 
-    load("up", up_hbm, up_v)
+    bands = [pl.ds(j * HD, HD) for j in range(tokens // HD)]
+    for j, band in enumerate(bands):
+        load(f"up{j}", up_hbm.at[band], up_v.at[band])
     load("len", len_hbm, len_ref)
 
     def w_rows(index, part):
         return w_all.at[block(index, 0 if part == "A" else half, half)]
 
-    locals_["up"].wait()
-    for j in range(up_v.shape[1] // HD):
-        up_t[j * HD:(j + 1) * HD, :] = up_v[:, j * HD:(j + 1) * HD].T
+    for j, band in enumerate(bands):
+        locals_[f"up{j}"].wait()
+        up_t[:, band] = up_v[band, :].T
     g_all[0, block(tau), :] = up_t[block(x), :]
     pl.semaphore_wait(barrier, len(peers))
 

time: 44.1 us -> 44 us (level)
  no operation moved by 1% of the time
where the time goes in v5:
time: 44 us; the launch traced here: 43.6 us
  Pallas kernels  42.9 us (98%)
  between operations  0.64 us (1%)
    pallas_call x1, Pallas kernels, per_device(): pl.pallas_call(kernel, out_shape=[pltpu.VMEM(*shape) for shape in shapes]...  41.9 us
    pallas_call x1, Pallas kernels, per_device(): pl.pallas_call(copy_kernel, out_shape=[pltpu.HBM(*shape) for shape in sha...  1.05 us

profile of v5, /device:TPU:32, one launch (start us, length us, event | category | flops | bytes accessed | tf_op | source)
XLA Modules:
  0.0 43.6 jit_solution(6344252933046818880)
XLA Ops:
  0.6 41.9 %shard_map.110 = (bf16[256,384]{1,0:T(8,128)(2,1)S(1)}, bf16[256,384]{1,0:T(8,128)(2,1)S(1)}, bf16[256,384]{1,0:T(8,128)(2,1)S(1)}, f32[192,384]{1,0:T(8,128)S(1)}, f32[192,384]{1,0:T(8,128)S(1)}) custom-call(s32[1,8]{1,0:T(1,128)} %len_hbm.1, bf16[256,384]{1,0:T(8,128)(2,1)} %q_hbm.1, bf16[256,384]{1,0:T(8,128)(2,1)} %k_hbm.1, bf16[256,384]{1,0:T(8,128)(2,1)} %v_hbm.1, ...), custom_call_target="tpu_custom_call" | custom-call | tf_op jit(solution)/shard_map/pallas_call | solution.py:391
  42.5 1.1 %shard_map.111 = (bf16[256,384]{1,0:T(8,128)(2,1)}, bf16[256,384]{1,0:T(8,128)(2,1)}, bf16[256,384]{1,0:T(8,128)(2,1)}, f32[192,384]{1,0:T(8,128)}, f32[192,384]{1,0:T(8,128)}) custom-call(bf16[256,384]{1,0:T(8,128)(2,1)S(1)} %get-tuple-element.10.refs_0_, bf16[256,384]{1,0:T(8,128)(2,1)S(1)} %get-tuple-element.11.refs_1_, ...), custom_call_target="tpu_custom_call" | custom-call | tf_op jit(solution)/shard_map/pallas_call | solution.py:401

commit v6 on v5

--- a/solution.py
+++ b/solution.py
@@ -143,7 +143,12 @@
         piece = g_rows(slot, 0, part)
         send(f"y{slot}+{part}", piece, piece, at(dy=1))
         send(f"y{slot}-{part}", piece, piece, at(dy=-1))
-        send(f"s{slot}0{part}", piece, piece, at(other=True))
+        to_other(slot, 0, "0", part)
+
+    def to_other(slot, dy, name, part):
+        if part == H - 1:
+            whole = g_all.at[slot, block(((y + dy + NY) % NY) * 2 + c)]
+            send(f"s{slot}{name}", whole, whole, at(other=True))
 
     def relay_y(slot, sign, part):
         arrive(f"y{slot}{sign}{part}")
@@ -151,12 +156,11 @@
         piece = g_rows(slot, -one, part)
         if (part < H // 2) == (sign == "+"):
             send(f"y{slot}{sign}{part}F", piece, piece, at(dy=one))
-        send(f"s{slot}{sign}{part}", piece, piece, at(other=True))
+        to_other(slot, -one, sign, part)
 
     def end_y(slot, part):
         arrive(f"y{slot}{'+' if part < H // 2 else '-'}{part}F")
-        piece = g_rows(slot, 2, part)
-        send(f"s{slot}3{part}", piece, piece, at(other=True))
+        to_other(slot, 2, "3", part)
 
     def end_core(slot):
         all_of("g", g_all.at[slot, pl.ds(0, 4 * rows)], f"s{slot}").wait_recv()
@@ -331,11 +335,11 @@
         else:
             end_z()
 
-    pieces = len(senders["g"]) * piece_rows // NX
+    blocks = (NX - 1) + NX * (2 + 1 + NY)
     for kind, ref in (
         ("w", w_all.at[pl.ds(0, len(senders["w"]) * half)]),
         ("c", cnt_z.at[pl.ds(0, len(senders["c"]))]),
-        ("g", g_all.at[:, pl.ds(0, pieces)]),
+        ("g", g_all.at[:, pl.ds(0, blocks * rows // NX)]),
         ("a", att_t.at[pl.ds(0, NX - 1)]),
         ("r", xs.at[pl.ds(0, NX - 1)]),
         ("x", cnt_x.at[pl.ds(0, NX - 1)]),

time: 44 us -> 44.1 us (level)
  no operation moved by 1% of the time
where the time goes in v6:
time: 44.1 us; the launch traced here: 43.6 us
  Pallas kernels  42.9 us (97%)
  between operations  0.64 us (1%)
    pallas_call x1, Pallas kernels, per_device(): pl.pallas_call(kernel, out_shape=[pltpu.VMEM(*shape) for shape in shapes]...  41.9 us
    pallas_call x1, Pallas kernels, per_device(): pl.pallas_call(copy_kernel, out_shape=[pltpu.HBM(*shape) for shape in sha...  1.05 us

profile of v6, /device:TPU:32, one launch (start us, length us, event | category | flops | bytes accessed | tf_op | source)
XLA Modules:
  0.0 43.6 jit_solution(6997548191010758394)
XLA Ops:
  0.6 41.9 %shard_map.110 = (bf16[256,384]{1,0:T(8,128)(2,1)S(1)}, bf16[256,384]{1,0:T(8,128)(2,1)S(1)}, bf16[256,384]{1,0:T(8,128)(2,1)S(1)}, f32[192,384]{1,0:T(8,128)S(1)}, f32[192,384]{1,0:T(8,128)S(1)}) custom-call(s32[1,8]{1,0:T(1,128)} %len_hbm.1, bf16[256,384]{1,0:T(8,128)(2,1)} %q_hbm.1, bf16[256,384]{1,0:T(8,128)(2,1)} %k_hbm.1, bf16[256,384]{1,0:T(8,128)(2,1)} %v_hbm.1, ...), custom_call_target="tpu_custom_call" | custom-call | tf_op jit(solution)/shard_map/pallas_call | solution.py:395
  42.5 1.1 %shard_map.111 = (bf16[256,384]{1,0:T(8,128)(2,1)}, bf16[256,384]{1,0:T(8,128)(2,1)}, bf16[256,384]{1,0:T(8,128)(2,1)}, f32[192,384]{1,0:T(8,128)}, f32[192,384]{1,0:T(8,128)}) custom-call(bf16[256,384]{1,0:T(8,128)(2,1)S(1)} %get-tuple-element.10.refs_0_, bf16[256,384]{1,0:T(8,128)(2,1)S(1)} %get-tuple-element.11.refs_1_, ...), custom_call_target="tpu_custom_call" | custom-call | tf_op jit(solution)/shard_map/pallas_call | solution.py:405
